TPU v7x, 32 devices: a whole 2x2x4 slice. The times are simulated.
32 devices in a mesh: section: 2 (over core), fsdp: 4 (over y, x), replica: 4 (over z).
Axes of the slice: x: 2, y: 2, z: 4, core: 2. Of those that a mesh axis runs over, the one named last changes fastest.
Arguments:
- ends_in: bfloat16 [2, 320, 197, 384], P('section', ('fsdp', 'replica')), may hold values from -6 to 6
- live: int32 [2, 16], P(None, ('fsdp', 'replica')), may hold values from 9 to 10, as said below
- gain_attn: bfloat16 [2, 384], P('section', 'fsdp'), may hold values from 0.25 to 1.75
- w_qkv: bfloat16 [2, 384, 1152], P('section', 'fsdp'), may hold values from -0.4375 to 0.4375
- w_out: bfloat16 [2, 384, 384], P('section', 'fsdp'), may hold values from -0.875 to 0.875
- gain_mlp: bfloat16 [2, 384], P('section', 'fsdp'), may hold values from 0.25 to 1.75
- w_up: bfloat16 [2, 384, 1536], P('section', 'fsdp'), may hold values from -0.3125 to 0.3125
- w_down: bfloat16 [2, 1536, 384], P('section', 'fsdp'), may hold values from -0.21875 to 0.21875
Outputs:
- ends_out: bfloat16 [2, 320, 197, 384], P('section', ('fsdp', 'replica'))
- grad_gain_attn: float32 [2, 384], P('section', 'fsdp')
- grad_w_qkv: float32 [2, 384, 1152], P('section', 'fsdp')
- grad_w_out: float32 [2, 384, 384], P('section', 'fsdp')
- grad_gain_mlp: float32 [2, 384], P('section', 'fsdp')
- grad_w_up: float32 [2, 384, 1536], P('section', 'fsdp')
- grad_w_down: float32 [2, 1536, 384], P('section', 'fsdp')
Inputs may be any that keep to these rules, and one draw needn't show every extreme that they name: live[m, d] is the number of live images among the 10 slots of device d in micro-batch m; they are its first slots, the rest are padding.
All inputs are finite; a program needn't handle non-finite values.
Results may differ from a plain program's by a relative error of at most 0.03.
The roundings to bfloat16 on the way count: a program that leaves them out, or rounds other values in their place, can miss the bound.
Values may be sent and summed in bfloat16 or wider, within the bound.
No kernel may reach another device: no remote copies, remote signals or barrier semaphores. Data moves between devices by JAX's collectives and lax.ppermute only.
A program may use at most 512 MiB of HBM per device.

v0:
```python
import jax
import jax.numpy as jnp
from jax import lax
from jax.sharding import PartitionSpec as P

HEADS = 6
HEAD_DIM = 64


EPS = 1e-06
ROOT_HALF = 0.7071067811865476
INV_ROOT_TWO_PI = 0.3989422804014327


def from_behind(value, axis, by):
    size = lax.axis_size(axis)
    pairs = [(i, i + by) for i in range(size) if 0 <= i + by < size]
    return lax.ppermute(value, axis, pairs)


def shortened(value):

    def short(part):
        return part.astype(jnp.bfloat16) if part.dtype == jnp.float32 else part

    return jax.tree.map(short, value)


def normalize(values, gain_vec):
    row_mean = jnp.mean(values, axis=-1, keepdims=True)
    centered = values - row_mean
    row_scale = lax.rsqrt(jnp.mean(centered * centered, axis=-1, keepdims=True) + EPS)
    normed = centered * row_scale
    return (normed, row_scale, (normed * gain_vec).astype(jnp.bfloat16))


def norm_back(grad_entry, normed, row_scale, gain_vec):
    grad_normed = grad_entry * gain_vec
    inner_term = grad_normed - jnp.mean(grad_normed, axis=-1, keepdims=True)
    inner_term = inner_term - normed * jnp.mean(grad_normed * normed, axis=-1, keepdims=True)
    return (row_scale * inner_term, jnp.sum(grad_entry * normed, axis=(0, 1)))


def project(left_side, right_side):
    return jnp.einsum("bsk,kn->bsn", left_side, right_side, preferred_element_type=jnp.float32)


def weight_grad(left_side, right_side):
    return jnp.einsum("bsk,bsn->kn", left_side, right_side, preferred_element_type=jnp.float32)


def back_project(grad_rows, right_side):
    return jnp.einsum("bsn,kn->bsk", grad_rows, right_side, preferred_element_type=jnp.float32)


def layer_forward(inputs, weights):
    gain_one, qkv_matrix, out_matrix, gain_two, up_matrix, down_matrix = weights
    image_count, length, model_width = inputs.shape
    normed_one, scale_one, entry_one = normalize(inputs, gain_one)
    joint_qkv = project(entry_one, qkv_matrix).astype(jnp.bfloat16)
    joint_qkv = joint_qkv.reshape(image_count, length, 3, HEADS, HEAD_DIM)
    queries = joint_qkv[:, :, 0]
    key_rows = joint_qkv[:, :, 1]
    values = joint_qkv[:, :, 2]
    scores = jnp.einsum(
        "bqhd,bkhd->bhqk", queries, key_rows, preferred_element_type=jnp.float32
    ) * HEAD_DIM ** (-0.5)
    attn_probs = jax.nn.softmax(scores, axis=-1)
    mixed_heads = jnp.einsum(
        "bhqk,bkhd->bqhd",
        attn_probs.astype(jnp.bfloat16),
        values,
        preferred_element_type=jnp.float32,
    )
    mixed_heads = mixed_heads.reshape(image_count, length, model_width).astype(jnp.bfloat16)
    middle = inputs + project(mixed_heads, out_matrix)
    normed_two, scale_two, entry_two = normalize(middle, gain_two)
    hidden = project(entry_two, up_matrix)
    active = (hidden * 0.5 * (1.0 + lax.erf(hidden * ROOT_HALF))).astype(jnp.bfloat16)
    result = middle + project(active, down_matrix)
    kept = (
        normed_one,
        scale_one,
        entry_one,
        queries,
        key_rows,
        values,
        attn_probs,
        mixed_heads,
        normed_two,
        scale_two,
        entry_two,
        hidden,
        active,
    )
    return (result, kept)


def layer_backward(cotangent, kept, weights):
    gain_one, qkv_matrix, out_matrix, gain_two, up_matrix, down_matrix = weights
    (
        normed_one,
        scale_one,
        entry_one,
        queries,
        key_rows,
        values,
        attn_probs,
        mixed_heads,
        normed_two,
        scale_two,
        entry_two,
        hidden,
        active,
    ) = kept
    image_count, length, model_width = cotangent.shape
    grad_low = cotangent.astype(jnp.bfloat16)
    grad_down = weight_grad(active, grad_low)
    grad_active = back_project(grad_low, down_matrix)
    gelu_cdf = 0.5 * (1.0 + lax.erf(hidden * ROOT_HALF))
    gelu_slope = gelu_cdf + hidden * jnp.exp(-0.5 * hidden * hidden) * INV_ROOT_TWO_PI
    grad_hidden = (grad_active * gelu_slope).astype(jnp.bfloat16)
    grad_up = weight_grad(entry_two, grad_hidden)
    grad_entry_two = back_project(grad_hidden, up_matrix)
    grad_norm_two, grad_gain_two = norm_back(grad_entry_two, normed_two, scale_two, gain_two)
    grad_middle = cotangent + grad_norm_two
    middle_low = grad_middle.astype(jnp.bfloat16)
    grad_out = weight_grad(mixed_heads, middle_low)
    grad_mixed = back_project(middle_low, out_matrix).astype(jnp.bfloat16)
    grad_mixed = grad_mixed.reshape(image_count, length, HEADS, HEAD_DIM)
    grad_probs = jnp.einsum(
        "bqhd,bkhd->bhqk", grad_mixed, values, preferred_element_type=jnp.float32
    )
    grad_values = jnp.einsum(
        "bhqk,bqhd->bkhd",
        attn_probs.astype(jnp.bfloat16),
        grad_mixed,
        preferred_element_type=jnp.float32,
    )
    row_total = jnp.sum(grad_probs * attn_probs, axis=-1, keepdims=True)
    grad_scores = (attn_probs * (grad_probs - row_total)).astype(jnp.bfloat16)
    grad_queries = jnp.einsum(
        "bhqk,bkhd->bqhd", grad_scores, key_rows, preferred_element_type=jnp.float32
    ) * HEAD_DIM ** (-0.5)
    grad_keys = jnp.einsum(
        "bhqk,bqhd->bkhd", grad_scores, queries, preferred_element_type=jnp.float32
    ) * HEAD_DIM ** (-0.5)
    grad_joint = jnp.stack([grad_queries, grad_keys, grad_values], axis=2).astype(jnp.bfloat16)
    grad_joint = grad_joint.reshape(image_count, length, 3 * model_width)
    grad_qkv = weight_grad(entry_one, grad_joint)
    grad_entry_one = back_project(grad_joint, qkv_matrix)
    grad_norm_one, grad_gain_one = norm_back(grad_entry_one, normed_one, scale_one, gain_one)
    grad_input = grad_middle + grad_norm_one
    return (grad_input, (grad_gain_one, grad_qkv, grad_out, grad_gain_two, grad_up, grad_down))


def local(ends_in, live, gain_attn, w_qkv, w_out, gain_mlp, w_up, w_down):
    gathered = (
        lax.all_gather(gain_attn, "fsdp", axis=1, tiled=True),
        lax.all_gather(w_qkv, "fsdp", axis=1, tiled=True),
        lax.all_gather(w_out, "fsdp", axis=1, tiled=True),
        lax.all_gather(gain_mlp, "fsdp", axis=1, tiled=True),
        lax.all_gather(w_up, "fsdp", axis=1, tiled=True),
        lax.all_gather(w_down, "fsdp", axis=1, tiled=True),
    )
    weights = (
        gathered[0][0].astype(jnp.float32),
        gathered[1][0],
        gathered[2][0],
        gathered[3][0].astype(jnp.float32),
        gathered[4][0],
        gathered[5][0],
    )
    micro_count = live.shape[0]
    slot_count = ends_in.shape[1] // micro_count
    own_rows = ends_in[0].reshape(micro_count, slot_count, ends_in.shape[2], ends_in.shape[3])
    section_idx = lax.axis_index("section")
    is_first = section_idx == 0
    slot_ids = jnp.arange(slot_count, dtype=jnp.int32)
    live_mask = (slot_ids[None, :] < live).astype(jnp.float32)

    def run_forward(entering):
        result, kept = layer_forward(entering.astype(jnp.float32), weights)
        return (result, kept)

    def skip_forward(entering):
        return jax.tree.map(jnp.zeros_like, run_forward(entering))

    def run_backward(cotangent, early_store, late_store):
        stored = lax.cond(is_first, lambda: early_store, lambda: late_store)
        return layer_backward(cotangent, stored, weights)

    def skip_backward(cotangent, early_store, late_store):
        return jax.tree.map(jnp.zeros_like, run_backward(cotangent, early_store, late_store))

    received = jnp.zeros_like(own_rows[0])
    results = []
    stores = []
    for tick_step in range(micro_count + 1):
        entering = jnp.where(is_first, own_rows[min(tick_step, micro_count - 1)], received)
        busy = jnp.logical_and(tick_step - section_idx >= 0, tick_step - section_idx < micro_count)
        result, stored = lax.cond(busy, run_forward, skip_forward, entering)
        results.append(result)
        stores.append(stored)
        if tick_step < micro_count:
            received = from_behind(result.astype(jnp.bfloat16), "section", 1)
    received_grad = jnp.zeros_like(own_rows[0])
    leaving = []
    grad_totals = None
    for tick_step in range(micro_count + 1):
        early_idx = max(tick_step - 1, 0)
        late_idx = min(tick_step + 1, micro_count)
        batch_idx = min(tick_step, micro_count - 1)
        own_grad = own_rows[batch_idx].astype(jnp.float32) * live_mask[batch_idx][:, None, None]
        cotangent = jnp.where(is_first, received_grad.astype(jnp.float32), own_grad)
        busy = jnp.logical_and(
            tick_step - 1 + section_idx >= 0, tick_step - 1 + section_idx < micro_count
        )
        grad_input, layer_grads = lax.cond(
            busy, run_backward, skip_backward, cotangent, stores[early_idx], stores[late_idx]
        )
        leaving.append(grad_input)
        grad_totals = (
            layer_grads if grad_totals is None else jax.tree.map(jnp.add, grad_totals, layer_grads)
        )
        if tick_step < micro_count:
            received_grad = from_behind(grad_input.astype(jnp.bfloat16), "section", -1)
    out_rows = []
    for batch_idx in range(micro_count):
        masked_out = results[batch_idx + 1] * live_mask[batch_idx][:, None, None]
        out_rows.append(jnp.where(is_first, leaving[batch_idx + 1], masked_out))
    ends_out = jnp.stack(out_rows).reshape(ends_in.shape).astype(jnp.bfloat16)
    local_grads = tuple((member[None] for member in grad_totals))
    shards = jax.tree.map(
        lambda part: part.astype(jnp.float32),
        lax.psum_scatter(shortened(local_grads), "fsdp", scatter_dimension=1, tiled=True),
    )
    summed = jax.tree.map(
        lambda part: part.astype(jnp.float32), lax.psum(shortened(shards), "replica")
    )
    return (ends_out, summed[0], summed[1], summed[2], summed[3], summed[4], summed[5])


def solution(mesh):
    in_specs = (
        P("section", ("fsdp", "replica"), None, None),
        P(None, ("fsdp", "replica")),
        P("section", "fsdp"),
        P("section", "fsdp", None),
        P("section", "fsdp", None),
        P("section", "fsdp"),
        P("section", "fsdp", None),
        P("section", "fsdp", None),
    )
    out_specs = (
        P("section", ("fsdp", "replica"), None, None),
        P("section", "fsdp"),
        P("section", "fsdp", None),
        P("section", "fsdp", None),
        P("section", "fsdp"),
        P("section", "fsdp", None),
        P("section", "fsdp", None),
    )
    return jax.shard_map(local, mesh=mesh, in_specs=in_specs, out_specs=out_specs, check_vma=False)
```

profile of v0, /device:TPU:13, one launch (start us, length us, event | category | flops | bytes accessed | tf_op | source)
XLA Modules:
  0.0 1037.9 jit_solution(2586146821199038035)
XLA Ops:
  27.6 16.3 %all_gather.19 = bf16[1,384,1152]{2,1,0:T(8,128)(2,1)} all-gather(bf16[1,96,1152]{2,1,0:T(8,128)(2,1)} %param.29), channel_id=1, replica_groups=mesh['section'=2,'fsdp'=4,'replica'=4] {'fsdp'}, dimensions={1}, use_global_device_ids=true | all-gather | bytes 1105920 | tf_op jit(solution)/shard_map/all_gather | solution.py:160
  47.2 25.1 %all-gather.5.cloned.1.call-done = bf16[1,1536,384]{2,1,0:T(8,128)(2,1)} async-done(((bf16[1,384,384]{2,1,0:T(8,128)(2,1)}), bf16[1,1536,384]{2,1,0:T(8,128)(2,1)}) %all-gather.5.cloned.1.call-update) | async-done | bytes 1179664 | tf_op jit(solution)/shard_map/all_gather | solution.py:164
  72.3 30.6 %conditional.9 = (f32[10,197,384]{2,1,0:T(8,128)S(1)}, f32[10,197,384]{2,1,0:T(8,128)}, f32[10,197,1]{1,0,2:T(8,128)S(1)}, bf16[10,197,384]{2,1,0:T(8,128)(2,1)}...) conditional(s32[]{:T(128)} %convert_element_type.318, () %tuple.84, ...), branch_computations={%region_0.1_spmd, %region_1.8_spmd} | conditional | flops 7617296384 | bytes 159934448 | solution.py:202
  106.3 43.7 %collective-permute-done = bf16[10,197,384]{2,1,0:T(8,128)(2,1)} collective-permute-done((bf16[10,197,384]{2,1,0:T(8,128)(2,1)}, bf16[10,197,384]{2,1,0:T(8,128)(2,1)}, u32[]{:S(2)}, u32[]{:S(2)}) %collective-permute-start) | collective-permute-done | bytes 1512992 | tf_op jit(solution)/shard_map/ppermute | solution.py:18
  150.0 76.8 %conditional.10 = (f32[10,197,384]{2,1,0:T(8,128)S(1)}, f32[10,197,384]{2,1,0:T(8,128)}, f32[10,197,1]{1,0,2:T(8,128)S(1)}, bf16[10,197,384]{2,1,0:T(8,128)(2,1)...) conditional(s32[]{:T(128)} %convert_element_type.317, () %tuple.83, ...), branch_computations={%region_8.9_spmd, %region_9.16_spmd} | conditional | flops 7615027200 | bytes 156908496 | solution.py:202
  231.7 149.2 %conditional.11 = (bf16[10,197,384]{2,1,0:T(8,128)(2,1)}, f32[384]{0:T(512)}, f32[384,1152]{1,0:T(8,128)}, f32[384,384]{1,0:T(8,128)}, f32[384]{0:T(512)}, /*index=5*/f32[384,1536]{1,0:T(8,128)}, f32[1536,384]{1,0:T(8,128)}) conditional(s32[]{:T(128)} %convert_element_type.315, () %tuple.82, (pred[]{:T(512)}, bf16[10,197,384]{2,1,0:T(8,128)(2,1)S(1)}, ...), branch_computations={%region_24.25_spmd, %region_25.35_spmd} | conditional | flops 15214668800 | bytes 491462912 | solution.py:219
  232.4 55.3 %conditional = (f32[10,197,384]{2,1,0:T(8,128)}, f32[10,197,1]{1,2,0:T(1,128)}, bf16[10,197,384]{2,1,0:T(8,128)(2,1)}, f32[10,6,197,197]{3,2,1,0:T(8,128)}, bf16...) conditional(s32[]{:T(128)} %convert_element_type.253, ...), branch_computations={%region_26.26_spmd, %region_27.27_spmd} | conditional | bytes 91282056 | solution.py:190
  263.9 13.8 %copy.326 = f32[10,6,197,197]{3,2,1,0:T(8,128)} copy(f32[10,6,197,197]{2,3,1,0:T(8,128)} %get-tuple-element.1304) | data formatting | bytes 18628320 | tf_op jit(solution)/shard_map
  331.4 13.8 %copy.222 = f32[10,6,197,197]{2,3,1,0:T(8,128)} copy(f32[10,6,197,197]{3,2,1,0:T(8,128)} %get-tuple-element.590) | data formatting | bytes 18628320 | tf_op jit(solution)/shard_map/cond/branch_1_fun/cond | solution.py:190
  345.1 11.7 %multiply_reduce_fusion.6 = (f32[10,6,197]{2,1,0:T(8,128)S(1)}, f32[10,6,197,197]{2,3,1,0:T(8,128)}) fusion(f32[10,6,197,197]{2,3,1,0:T(8,128)} %copy.222, bf16[10,197,6,64]{1,3,2,0:T(8,128)(2,1)S(1)} %bitcast.353, bf16[10,197,6,64]{1,3,2,0:T(8,128)(2,1)} %get-tuple-element.1298), kind=kOutput, calls=%fused_computation.125 | convolution fusion | flops 302698368 | bytes 21701520 | tf_op jit(solution)/shard_map/cond/branch_1_fun/bqhd,bkhd->bhqk/dot_general | solution.py:131
  385.6 79.1 %conditional.12 = (f32[10,197,384]{2,1,0:T(8,128)S(1)}, f32[10,197,384]{2,1,0:T(8,128)}, f32[10,197,1]{1,0,2:T(8,128)S(1)}, bf16[10,197,384]{2,1,0:T(8,128)(2,1)...) conditional(s32[]{:T(128)} %convert_element_type.327, () %tuple.88, ...), branch_computations={%region_16.17_spmd, %region_17.24_spmd} | conditional | flops 7615027200 | bytes 153369520 | solution.py:202
  412.4 11.7 %fusion.145 = (f32[10,6,197]{2,1,0:T(8,128)}, f32[10,6,197,197]{2,3,1,0:T(8,128)}) fusion(bf16[10,197,6,64]{1,3,2,0:T(8,128)(2,1)} %get-tuple-element.1675, bf16[10,197,6,64]{1,3,2,0:T(8,128)(2,1)} %get-tuple-element.1676), kind=kOutput, calls=%fused_computation.282 | convolution fusion | flops 305038912 | bytes 12387360 | tf_op jit(solution)/shard_map/cond/branch_1_fun/sub | solution.py:68
  469.1 162.1 %conditional.13 = (bf16[10,197,384]{2,1,0:T(8,128)(2,1)}, f32[384]{0:T(512)S(1)}, f32[384,1152]{1,0:T(8,128)}, f32[384,384]{1,0:T(8,128)}, f32[384]{0:T(512)S(1)...) conditional(s32[]{:T(128)} %convert_element_type.314, () %tuple.81, (pred[]{:T(512)}, f32[10,197,384]{2,1,0:T(8,128)}, ...), branch_computations={%region_35.36_spmd, %region_36.46_spmd} | conditional | flops 15210886144 | bytes 419186720 | solution.py:219
  469.1 56.0 %conditional.1 = (f32[10,197,384]{2,1,0:T(8,128)}, f32[10,197,1]{1,2,0:T(1,128)S(1)}, bf16[10,197,384]{2,1,0:T(8,128)(2,1)}, f32[10,6,197,197]{3,2,1,0:T(8,128)}...) conditional(s32[]{:T(128)} %convert_element_type.261, ...), branch_computations={%region_37.37_spmd, %region_38.38_spmd} | conditional | bytes 85230184 | solution.py:190
  500.9 13.8 %copy.346 = f32[10,6,197,197]{3,2,1,0:T(8,128)} copy(f32[10,6,197,197]{2,3,1,0:T(8,128)} %get-tuple-element.1347) | data formatting | bytes 18628320 | tf_op jit(solution)/shard_map
  575.3 13.8 %copy.233 = f32[10,6,197,197]{2,3,1,0:T(8,128)} copy(f32[10,6,197,197]{3,2,1,0:T(8,128)} %get-tuple-element.638) | data formatting | bytes 18628320 | tf_op jit(solution)/shard_map/cond/branch_1_fun/cond | solution.py:190
  589.1 12.3 %multiply_reduce_fusion.13 = (f32[10,6,197]{2,1,0:T(8,128)S(1)}, f32[10,6,197,197]{2,3,1,0:T(8,128)}) fusion(f32[10,6,197,197]{2,3,1,0:T(8,128)} %copy.233, bf16[10,197,6,64]{1,3,2,0:T(8,128)(2,1)} %bitcast.355, bf16[10,197,6,64]{1,3,2,0:T(8,128)(2,1)} %get-tuple-element.1341), kind=kOutput, calls=%fused_computation.171 | convolution fusion | flops 302698368 | bytes 21701520 | tf_op jit(solution)/shard_map/cond/branch_1_fun/bqhd,bkhd->bhqk/dot_general | solution.py:131
  668.1 158.6 %reduce-scatter.13.cloned.1.call-done = bf16[1,96,384]{2,1,0:T(8,128)(2,1)} async-done(((bf16[1,384,384]{2,1,0:T(8,128)(2,1)}), bf16[1,96,384]{2,1,0:T(8,128)(2,1)}) %reduce-scatter.13.cloned.1.call-update) | async-done | bytes 73744 | tf_op jit(solution)/shard_map/reduce_scatter | solution.py:236
  826.7 29.8 %reduce-scatter.11.cloned.1.call-done = bf16[1,96,1152]{2,1,0:T(8,128)(2,1)} async-done(((bf16[1,384,1152]{2,1,0:T(8,128)(2,1)}), bf16[1,96,1152]{2,1,0:T(8,128)(2,1)}) %reduce-scatter.11.cloned.1.call-update) | async-done | bytes 221200 | tf_op jit(solution)/shard_map/reduce_scatter | solution.py:236
  856.5 31.9 %reduce-scatter.15.cloned.1.call-done = bf16[1,96,1536]{2,1,0:T(8,128)(2,1)} async-done(((bf16[1,384,1536]{2,1,0:T(8,128)(2,1)}), bf16[1,96,1536]{2,1,0:T(8,128)(2,1)}) %reduce-scatter.15.cloned.1.call-update) | async-done | bytes 294928 | tf_op jit(solution)/shard_map/reduce_scatter | solution.py:236
  888.4 31.3 %reduce-scatter.17.cloned.1.call-done = bf16[1,384,384]{2,1,0:T(8,128)(2,1)} async-done(((bf16[1,1536,384]{2,1,0:T(8,128)(2,1)}), bf16[1,384,384]{2,1,0:T(8,128)(2,1)}) %reduce-scatter.17.cloned.1.call-update) | async-done | bytes 294928 | tf_op jit(solution)/shard_map/reduce_scatter | solution.py:236
  924.3 22.2 %reduce-scatter.19.cloned.1.call-done = bf16[96,1]{1,0:T(8,128)(2,1)} async-done(((bf16[384,1]{1,0:T(8,128)(2,1)}), bf16[96,1]{1,0:T(8,128)(2,1)}) %reduce-scatter.19.cloned.1.call-update) | async-done | bytes 208
  947.3 26.5 %reduce-scatter.21.cloned.1.call-done = bf16[96,1]{1,0:T(8,128)(2,1)} async-done(((bf16[384,1]{1,0:T(8,128)(2,1)}), bf16[96,1]{1,0:T(8,128)(2,1)}) %reduce-scatter.21.cloned.1.call-update) | async-done | bytes 208
  982.6 41.7 %all-reduce.7.cloned.1.call-done = (bf16[1,96,1152]{2,1,0:T(8,128)(2,1)}, bf16[1,96,384]{2,1,0:T(8,128)(2,1)}, bf16[1,96,1536]{2,1,0:T(8,128)(2,1)}, bf16[1,384,384]{2,1,0:T(8,128)(2,1)}) async-done(((bf16[1,96,1152]{2,1,0:T(8,128)(2,1)}, bf16[1,96,384]{2,1,0:T(8,128)(2,1)}, bf16[1,96,1536]{2,1,0:T(8,128)(2,1)}, bf16[1,384,384]{2,1,0:T(8,128)(2,1)}), (bf16[1,96,1152]{2,1,0:T(8,128)(2,1)}, ...) | async-done | bytes 884752 | tf_op jit(solution)/shard_map/psum | solution.py:239
  (312 shorter events, 506.0 us)
Async XLA Ops:
  7.2 40.0 %all-gather.3.cloned.1.call-start = ((), (), s32[]{:S(2)}) async-start(), calls=%async_computation.6 | async-start | bytes 1474560 | tf_op jit(solution)/shard_map/all_gather | solution.py:163
  7.9 64.4 %all-gather.5.cloned.1.call-start = ((), (), s32[]{:S(2)}) async-start(), calls=%async_computation.7 | async-start | bytes 1474560 | tf_op jit(solution)/shard_map/all_gather | solution.py:164
  8.6 818.1 %reduce-scatter.13.cloned.1.call-start = ((), (), s32[]{:S(2)}) async-start(), calls=%async_computation.9 | async-start | bytes 368640 | tf_op jit(solution)/shard_map/reduce_scatter | solution.py:236
  19.2 212.4 %copy-start.60 = (f32[384]{0:T(512)}, f32[384]{0:T(512)S(1)}, u32[]{:S(2)}) copy-start(f32[384]{0:T(512)S(1)} %convert_element_type.353) | copy-start | bytes 4612
  27.6 204.0 %copy-start.35 = (bf16[1,384,384]{2,1,0:T(8,128)(2,1)}, bf16[1,384,384]{2,1,0:T(8,128)(2,1)S(1)}, u32[]{:S(2)}) copy-start(bf16[1,384,384]{2,1,0:T(8,128)(2,1)S(1)} %all_gather.20) | copy-start | bytes 884740
  102.9 128.8 %copy-start.11 = (bf16[10,197,384]{2,1,0:T(8,128)(2,1)}, bf16[10,197,384]{2,1,0:T(8,128)(2,1)S(1)}, u32[]{:S(2)}) copy-start(bf16[10,197,384]{2,1,0:T(8,128)(2,1)S(1)} %get-tuple-element.791) | copy-start | bytes 4538884
  104.4 45.6 %collective-permute-start = (bf16[10,197,384]{2,1,0:T(8,128)(2,1)}, bf16[10,197,384]{2,1,0:T(8,128)(2,1)}, u32[]{:S(2)}, u32[]{:S(2)}) collective-permute-start(bf16[10,197,384]{2,1,0:T(8,128)(2,1)} %convert_element_type.323), channel_id=1, source_target_pairs={{0,16},{1,17},{2,18},{3,19},{4,20},{5,21},{6,22},{7,23},{8,24},{9,... | collective-permute-start | bytes 4538888 | tf_op jit(solution)/shard_map/ppermute | solution.py:18
  106.3 123.5 %copy-start.66 = (f32[10]{0:T(128)}, f32[10]{0:T(128)S(1)}, u32[]{:S(2)}) copy-start(f32[10]{0:T(128)S(1)} %get-tuple-element.1508) | copy-start | bytes 124
  228.3 157.1 %collective-permute-start.2 = (bf16[10,197,384]{2,1,0:T(8,128)(2,1)}, bf16[10,197,384]{2,1,0:T(8,128)(2,1)}, u32[]{:S(2)}, u32[]{:S(2)}) collective-permute-start(bf16[10,197,384]{2,1,0:T(8,128)(2,1)} %convert_element_type.328), channel_id=1, source_target_pairs={{0,16},{1,17},{2,18},{3,19},{4,20},{5,21},{6,22},{7,23},{8,24},{9,... | collective-permute-start | bytes 4538888 | tf_op jit(solution)/shard_map/ppermute | solution.py:18
  289.2 12.7 %slice-start = ((s8[6144000]{0:T(1024)(128)(4,1)}), s8[4194304]{0:T(1024)(128)(4,1)S(1)}, s32[]{:S(2)}) async-start(s8[6144000]{0:T(1024)(128)(4,1)} %bitcast.370), calls=%async_computation.15 | async-start | bytes 8388608 | tf_op jit(solution)/shard_map/cond
  291.6 10.3 slice-start.1
  345.1 11.7 %copy-start = (f32[10,6,197,197]{2,3,1,0:T(8,128)S(1)}, f32[10,6,197,197]{2,3,1,0:T(8,128)}, u32[]{:S(2)}) copy-start(f32[10,6,197,197]{2,3,1,0:T(8,128)} %copy.222) | copy-start | bytes 27942484 | tf_op jit(solution)/shard_map/cond
  381.0 83.8 %collective-permute-start.1 = (bf16[10,197,384]{2,1,0:T(8,128)(2,1)}, bf16[10,197,384]{2,1,0:T(8,128)(2,1)}, u32[]{:S(2)}, u32[]{:S(2)}) collective-permute-start(bf16[10,197,384]{2,1,0:T(8,128)(2,1)} %get-tuple-element.794), channel_id=1, source_target_pairs={{16,0},{17,1},{18,2},{19,3},{20,4},{21,5},{22,6},{23,7},{24,8},{25... | collective-permute-start | bytes 4538888 | tf_op jit(solution)/shard_map/ppermute | solution.py:18
  448.9 10.2 copy-start.71
  589.1 12.3 %copy-start.1 = (f32[10,6,197,197]{2,3,1,0:T(8,128)S(1)}, f32[10,6,197,197]{2,3,1,0:T(8,128)}, u32[]{:S(2)}) copy-start(f32[10,6,197,197]{2,3,1,0:T(8,128)} %copy.233) | copy-start | bytes 27942484 | tf_op jit(solution)/shard_map/cond
  631.2 4.7 collective-permute-start.3
  651.8 204.7 %reduce-scatter.11.cloned.1.call-start = ((), (), s32[]{:S(2)}) async-start(), calls=%async_computation.8 | async-start | bytes 1105920 | tf_op jit(solution)/shard_map/reduce_scatter | solution.py:236
  655.6 232.8 %reduce-scatter.15.cloned.1.call-start = ((), (), s32[]{:S(2)}) async-start(), calls=%async_computation.10 | async-start | bytes 1474560 | tf_op jit(solution)/shard_map/reduce_scatter | solution.py:236
  660.4 259.4 %reduce-scatter.17.cloned.1.call-start = ((), (), s32[]{:S(2)}) async-start(), calls=%async_computation.11 | async-start | bytes 1474560 | tf_op jit(solution)/shard_map/reduce_scatter | solution.py:236
  660.4 259.4 %copy-start.17 = (f32[10,197,384]{2,1,0:T(8,128)S(1)}, f32[10,197,384]{2,1,0:T(8,128)}, u32[]{:S(2)}) copy-start(f32[10,197,384]{2,1,0:T(8,128)} %copy-done.16) | copy-start | bytes 9077764
  660.4 259.4 %copy-start.67 = (f32[10]{0:T(128)S(1)}, f32[10]{0:T(128)}, u32[]{:S(2)}) copy-start(f32[10]{0:T(128)} %copy-done.66) | copy-start | bytes 124
  665.1 281.4 %reduce-scatter.19.cloned.1.call-start = ((), (), s32[]{:S(2)}) async-start(), calls=%async_computation.12 | async-start | bytes 122880
  666.6 307.2 %reduce-scatter.21.cloned.1.call-start = ((), (), s32[]{:S(2)}) async-start(), calls=%async_computation.13 | async-start | bytes 122880
  668.1 356.1 %all-reduce.7.cloned.1.call-start = ((), (), s32[]{:S(2)}) async-start(), calls=%async_computation.14 | async-start | bytes 1769472 | tf_op jit(solution)/shard_map/psum | solution.py:239
  (50 other events, 198.3 us)
Sparse Core Ops, SparseCore 0:
  9.8 33.0 all-gather.2
  44.7 27.4 all-gather.4
  652.0 174.7 reduce-scatter.12
  829.5 26.9 reduce-scatter.10
  859.9 28.5 reduce-scatter.14
  891.2 28.5 reduce-scatter.16
  923.1 23.3 reduce-scatter.18
  950.0 23.7 reduce-scatter.20
  976.5 47.7 all-reduce.6
where the time goes:
time: 1050 us; the launch traced here: 1040 us
  waiting for transfers between devices  414 us (39%)
  local copies, waits for them, and re-layouts  227 us (22%)
  matrix products  219 us (21%)
  other arithmetic  107 us (10%)
  blocking collectives  38.5 us (4%)
  between operations  15 us (1%)
    reduce_scatter x4, waiting for transfers between devices, local(): lax.psum_scatter(shortened(local_grads), 'fsdp', scatter_dimension=1, til...  252 us
    cond x104, local copies, waits for them, and re-layouts  79.1 us
    another operation x29, local copies, waits for them, and re-layouts  69.4 us
    unnamed x11, waiting for transfers between devices  50.2 us
    dot_general x8, matrix products, project(): jnp.einsum('bsk,kn->bsn', left_side, right_side, preferred_element_type=j...  49.4 us
    dot_general x8, matrix products, back_project(): jnp.einsum('bsn,kn->bsk', grad_rows, right_side, preferred_element_type=j...  47 us
    ppermute x4, waiting for transfers between devices, from_behind(): return lax.ppermute(value, axis, pairs)  45.8 us
    psum x1, waiting for transfers between devices, local(): lax.psum(shortened(shards), 'replica')  41.7 us
  transfers between devices with their start and end apart: 13, of which 10 were waited for; matrix products, arithmetic and copies ran while one was open for 25% of the time, Pallas kernels for 0%

commit v1 on v0

v1 whole, which is shorter than its diff:
```python
import functools

import jax
import jax.numpy as jnp
from jax import lax
from jax.experimental import pallas as pl
from jax.experimental.pallas import tpu as pltpu
from jax.sharding import PartitionSpec as P

HEADS = 6
HEAD_DIM = 64
EPS = 1e-06
BF = jnp.bfloat16
F32 = jnp.float32
VMEM_LIMIT = 56 * 1024 * 1024
PER_STEP = 2
MOST_PIECES = 8


def dot_nn(a, b):
    return lax.dot_general(a, b, (((1,), (0,)), ((), ())), preferred_element_type=F32)


def dot_nt(a, b):
    return lax.dot_general(a, b, (((1,), (1,)), ((), ())), preferred_element_type=F32)


def norm_rows(values):
    centered = values - jnp.mean(values, axis=-1, keepdims=True)
    scale = lax.rsqrt(jnp.mean(centered * centered, axis=-1, keepdims=True) + EPS)
    return centered * scale, scale


def norm_rows_back(grad_normed, normed, scale):
    first = jnp.mean(grad_normed, axis=-1, keepdims=True)
    second = jnp.mean(grad_normed * normed, axis=-1, keepdims=True)
    return scale * (grad_normed - first - normed * second)


def gelu_both(v):
    cdf = 0.5 * (1.0 + lax.erf(v * 0.7071067811865476))
    density = jnp.exp(-0.5 * v * v) * 0.3989422804014327
    return v * cdf, cdf + v * density


def attn_fwd_kernel(length, x_ref, gain_ref, wqkv_ref, wout_ref,
                    qkv_ref, probs_ref, mixt_ref, mid_ref, entry_s, qkv_s, mixed_s):
    images, rows, width = x_ref.shape
    for g in range(images):
        normed, _ = norm_rows(x_ref[g].astype(F32))
        entry_s[g * rows:(g + 1) * rows, :] = (normed * gain_ref[...]).astype(BF)
    joint = dot_nn(entry_s[...], wqkv_ref[...]).astype(BF)
    qkv_s[...] = joint
    lane = lax.broadcasted_iota(jnp.int32, (rows, 2 * HEAD_DIM), 1)
    cut = (length // 8) * 8
    tail_row = lax.broadcasted_iota(jnp.int32, (rows - cut, rows), 0) + cut
    for g in range(images):
        qkv_ref[g] = qkv_s[g * rows:(g + 1) * rows, :]
        for pair in range(HEADS // 2):
            at = pair * 2 * HEAD_DIM
            q = qkv_s[g * rows:(g + 1) * rows, at:at + 2 * HEAD_DIM] * 0.125
            k = qkv_s[g * rows:(g + 1) * rows, width + at:width + at + 2 * HEAD_DIM]
            v = qkv_s[g * rows:(g + 1) * rows, 2 * width + at:2 * width + at + 2 * HEAD_DIM]
            v_t = v.T
            for side in range(2):
                own = (lane // HEAD_DIM) == side
                scores = dot_nt(k, jnp.where(own, q, jnp.zeros_like(q)))
                tail = jnp.where(tail_row < length, scores[cut:], -1e30)
                top = jnp.maximum(jnp.max(scores[:cut], axis=0, keepdims=True),
                                  jnp.max(tail, axis=0, keepdims=True))
                e_top = jnp.exp(scores[:cut] - top)
                e_tail = jnp.exp(tail - top)
                total = jnp.sum(e_top, axis=0, keepdims=True) + jnp.sum(e_tail, axis=0, keepdims=True)
                inv = 1.0 / total
                head = pair * 2 + side
                probs = jnp.concatenate([e_top * inv, e_tail * inv], axis=0).astype(BF)
                probs_ref[g, head] = probs
                mixed = dot_nn(v_t[side * HEAD_DIM:(side + 1) * HEAD_DIM], probs)
                mixt_ref[g, head * HEAD_DIM:(head + 1) * HEAD_DIM, :] = mixed.astype(BF)
        mixed_s[g * rows:(g + 1) * rows, :] = mixt_ref[g].T
    added = dot_nn(mixed_s[...], wout_ref[...])
    for g in range(images):
        mid_ref[g] = x_ref[g].astype(F32) + added[g * rows:(g + 1) * rows]


def mlp_fwd_kernel(mid_ref, gain_ref, wup_ref, wdown_ref, out_ref, act_ref, slope_ref, entry_s, act_s):
    images, rows, width = mid_ref.shape
    for g in range(images):
        normed, _ = norm_rows(mid_ref[g])
        entry_s[g * rows:(g + 1) * rows, :] = (normed * gain_ref[...]).astype(BF)
    hidden_width = wup_ref.shape[1]
    step = 256
    for at in range(0, hidden_width, step):
        hidden = dot_nn(entry_s[...], wup_ref[:, at:at + step])
        act, slope = gelu_both(hidden)
        act_s[:, at:at + step] = act.astype(BF)
        for g in range(images):
            slope_ref[g, :, at:at + step] = slope[g * rows:(g + 1) * rows].astype(BF)
    added = dot_nn(act_s[...], wdown_ref[...])
    for g in range(images):
        act_ref[g] = act_s[g * rows:(g + 1) * rows, :]
        out_ref[g] = (mid_ref[g] + added[g * rows:(g + 1) * rows]).astype(BF)


def mlp_bwd_kernel(cot_ref, mid_ref, act_ref, slope_ref, gain_ref, wup_ref, wdown_ref,
                   gmid_ref, gup_ref, gdown_ref, up_acc, down_acc, entry_t, cot_t, gh_s):
    images, rows, width = mid_ref.shape
    step_id = pl.program_id(0)

    @pl.when(step_id == 0)
    def _():
        up_acc[...] = jnp.zeros_like(up_acc)
        down_acc[...] = jnp.zeros_like(down_acc)

    hidden_width = wup_ref.shape[1]
    step = 256
    for g in range(images):
        cot = cot_ref[g]
        normed, scale = norm_rows(mid_ref[g])
        entry = (normed * gain_ref[...]).astype(BF)
        entry_t[...] = entry.T
        cot_t[...] = cot.T
        for at in range(0, hidden_width, step):
            grad_act = dot_nt(cot, wdown_ref[at:at + step, :])
            gh_s[:, at:at + step] = (grad_act * slope_ref[g, :, at:at + step].astype(F32)).astype(BF)
        up_acc[...] += dot_nn(entry_t[...], gh_s[...])
        down_acc[...] += dot_nn(cot_t[...], act_ref[g])
        grad_entry = dot_nt(gh_s[...], wup_ref[...])
        back = norm_rows_back(grad_entry * gain_ref[...], normed, scale)
        gmid_ref[g] = cot.astype(F32) + back

    @pl.when(step_id == pl.num_programs(0) - 1)
    def _():
        gup_ref[...] = up_acc[...].astype(BF)
        for at in range(0, hidden_width, 128):
            gdown_ref[at:at + 128, :] = down_acc[:, at:at + 128].T.astype(BF)


def attn_bwd_kernel(gmid_ref, x_ref, qkv_ref, probs_ref, mixt_ref, gain_ref, wqkv_ref, wout_ref,
                    gx_ref, gqkv_ref, gout_ref, qkv_acc, out_acc, joint_s, entry_t):
    images, rows, width = x_ref.shape
    step_id = pl.program_id(0)

    @pl.when(step_id == 0)
    def _():
        qkv_acc[...] = jnp.zeros_like(qkv_acc)
        out_acc[...] = jnp.zeros_like(out_acc)

    lane = lax.broadcasted_iota(jnp.int32, (rows, 2 * HEAD_DIM), 1)
    for g in range(images):
        normed, scale = norm_rows(x_ref[g].astype(F32))
        entry_t[...] = (normed * gain_ref[...]).astype(BF).T
        low = gmid_ref[g].astype(BF)
        out_acc[...] += dot_nn(mixt_ref[g], low)
        grad_mixed = dot_nt(low, wout_ref[...]).astype(BF)
        grad_mixed_t = dot_nt(wout_ref[...], low).astype(BF)
        for pair in range(HEADS // 2):
            at = pair * 2 * HEAD_DIM
            q = qkv_ref[g, :, at:at + 2 * HEAD_DIM] * 0.125
            k = qkv_ref[g, :, width + at:width + at + 2 * HEAD_DIM]
            v = qkv_ref[g, :, 2 * width + at:2 * width + at + 2 * HEAD_DIM]
            k_t = (k * 0.125).T
            gm = grad_mixed[:, at:at + 2 * HEAD_DIM]
            grad_k = None
            grad_v = None
            grad_q_t = []
            for side in range(2):
                head = pair * 2 + side
                lo = head * HEAD_DIM
                own = (lane // HEAD_DIM) == side
                gm_own = jnp.where(own, gm, jnp.zeros_like(gm))
                q_own = jnp.where(own, q, jnp.zeros_like(q))
                probs = probs_ref[g, head]
                delta = jnp.sum(grad_mixed_t[lo:lo + HEAD_DIM].astype(F32)
                                * mixt_ref[g, lo:lo + HEAD_DIM, :].astype(F32), axis=0, keepdims=True)
                grad_probs = dot_nt(v, gm_own)
                grad_scores = (probs.astype(F32) * (grad_probs - delta)).astype(BF)
                part_v = dot_nn(probs, gm_own)
                part_k = dot_nn(grad_scores, q_own)
                grad_v = part_v if grad_v is None else grad_v + part_v
                grad_k = part_k if grad_k is None else grad_k + part_k
                grad_q_t.append(dot_nn(k_t[side * HEAD_DIM:(side + 1) * HEAD_DIM], grad_scores))
            grad_q = jnp.concatenate(grad_q_t, axis=0).astype(BF).T
            joint_s[:, at:at + 2 * HEAD_DIM] = grad_q
            joint_s[:, width + at:width + at + 2 * HEAD_DIM] = grad_k.astype(BF)
            joint_s[:, 2 * width + at:2 * width + at + 2 * HEAD_DIM] = grad_v.astype(BF)
        qkv_acc[...] += dot_nn(entry_t[...], joint_s[...])
        grad_entry = dot_nt(joint_s[...], wqkv_ref[...])
        back = norm_rows_back(grad_entry * gain_ref[...], normed, scale)
        gx_ref[g] = (gmid_ref[g] + back).astype(BF)

    @pl.when(step_id == pl.num_programs(0) - 1)
    def _():
        gqkv_ref[...] = qkv_acc[...].astype(BF)
        gout_ref[...] = out_acc[...].astype(BF)


def per_image(shape, g):
    return pl.BlockSpec((g,) + shape[1:], lambda i: (i,) + (0,) * (len(shape) - 1))


def whole(shape):
    return pl.BlockSpec(shape, lambda i: (0,) * len(shape))


def call(body, name, streams, fixed, stream_outs, fixed_outs, scratch, flops):
    images = streams[0].shape[0]
    g = PER_STEP if images % PER_STEP == 0 else 1
    outs = [jax.ShapeDtypeStruct(s, d) for s, d in stream_outs + fixed_outs]
    moved = sum(a.size * a.dtype.itemsize for a in list(streams) + list(fixed) + outs)
    return pl.pallas_call(
        body,
        name=name,
        grid=(images // g,),
        in_specs=[per_image(a.shape, g) for a in streams] + [whole(a.shape) for a in fixed],
        out_specs=[per_image(s, g) for s, _ in stream_outs] + [whole(s) for s, _ in fixed_outs],
        out_shape=outs,
        scratch_shapes=scratch(g),
        compiler_params=pltpu.CompilerParams(vmem_limit_bytes=VMEM_LIMIT, dimension_semantics=("arbitrary",)),
        cost_estimate=pl.CostEstimate(flops=int(flops), bytes_accessed=int(moved), transcendentals=0),
    )(*streams, *fixed)


def attn_fwd(x, length, gain, wqkv, wout):
    n, rows, width = x.shape
    return call(
        functools.partial(attn_fwd_kernel, length), "attention_forward", [x], [gain, wqkv, wout],
        [((n, rows, 3 * width), BF), ((n, HEADS, rows, rows), BF), ((n, width, rows), BF), ((n, rows, width), F32)],
        [],
        lambda g: [pltpu.VMEM((g * rows, width), BF), pltpu.VMEM((g * rows, 3 * width), BF), pltpu.VMEM((g * rows, width), BF)],
        2 * n * rows * width * 4 * width + 4 * n * rows * rows * width)


def mlp_fwd(mid, gain, wup, wdown):
    n, rows, width = mid.shape
    ff = wup.shape[1]
    return call(
        mlp_fwd_kernel, "mlp_forward", [mid], [gain, wup, wdown],
        [((n, rows, width), BF), ((n, rows, ff), BF), ((n, rows, ff), BF)], [],
        lambda g: [pltpu.VMEM((g * rows, width), BF), pltpu.VMEM((g * rows, ff), BF)],
        4 * n * rows * width * ff)


def mlp_bwd(cot, mid, act, slope, gain, wup, wdown):
    n, rows, width = mid.shape
    ff = wup.shape[1]
    return call(
        mlp_bwd_kernel, "mlp_backward", [cot, mid, act, slope], [gain, wup, wdown],
        [((n, rows, width), F32)], [((width, ff), BF), ((ff, width), BF)],
        lambda g: [pltpu.VMEM((width, ff), F32), pltpu.VMEM((width, ff), F32), pltpu.VMEM((width, rows), BF),
                   pltpu.VMEM((width, rows), BF), pltpu.VMEM((rows, ff), BF)],
        8 * n * rows * width * ff)


def attn_bwd(gmid, x, qkv, probs, mixt, gain, wqkv, wout):
    n, rows, width = x.shape
    return call(
        attn_bwd_kernel, "attention_backward", [gmid, x, qkv, probs, mixt], [gain, wqkv, wout],
        [((n, rows, width), BF)], [((width, 3 * width), BF), ((width, width), BF)],
        lambda g: [pltpu.VMEM((width, 3 * width), F32), pltpu.VMEM((width, width), F32),
                   pltpu.VMEM((rows, 3 * width), BF), pltpu.VMEM((width, rows), BF)],
        4 * n * rows * width * 4 * width + 10 * n * rows * rows * width)


def swap_section(value):
    return lax.ppermute(value, "section", [(0, 1), (1, 0)])


def pick(stack, index):
    return lax.dynamic_index_in_dim(stack, index, 0, keepdims=False)


def after(value, *others):
    return lax.optimization_barrier((value,) + others)[0]


def spread(value, axis):
    size = lax.axis_size(axis)
    me = lax.axis_index(axis)
    if size & (size - 1) or size > MOST_PIECES:
        return lax.all_gather(value, axis)
    full = jnp.zeros((size,) + value.shape, value.dtype)
    full = lax.dynamic_update_index_in_dim(full, value, me, 0)
    for k in range(1, size):
        piece = lax.ppermute(value, axis, [(i, i ^ k) for i in range(size)])
        full = lax.dynamic_update_index_in_dim(full, piece, me ^ k, 0)
    return full


def scatter_sum(stack, axis, dim):
    size = lax.axis_size(axis)
    me = lax.axis_index(axis)
    if size & (size - 1) or size > MOST_PIECES:
        return lax.psum_scatter(stack, axis, scatter_dimension=dim)
    total = lax.dynamic_index_in_dim(stack, me, dim, keepdims=False).astype(F32)
    for k in range(1, size):
        sent = lax.dynamic_index_in_dim(stack, me ^ k, dim, keepdims=False)
        total = total + lax.ppermute(sent, axis, [(i, i ^ k) for i in range(size)]).astype(F32)
    return total.astype(BF)


def all_sum(value, axis):
    size = lax.axis_size(axis)
    if size & (size - 1) or size > MOST_PIECES:
        return lax.psum(value, axis)
    total = value.astype(F32)
    for k in range(1, size):
        total = total + lax.ppermute(value, axis, [(i, i ^ k) for i in range(size)]).astype(F32)
    return total.astype(BF)


def gather_group(half, me):
    mine = spread(half, "fsdp")
    other = swap_section(mine)
    both = jnp.zeros((2,) + mine.shape, mine.dtype)
    both = lax.dynamic_update_index_in_dim(both, mine, me, 0)
    both = lax.dynamic_update_index_in_dim(both, other, 1 - me, 0)
    both = both.transpose(0, 2, 1, 3, 4)
    return both.reshape(2 * half.shape[0], -1, half.shape[2])


def reduce_group(halves, me):
    other = swap_section(pick(halves, 1 - me))
    chip = (pick(halves, me).astype(F32) + other.astype(F32)).astype(BF)
    return all_sum(scatter_sum(chip, "fsdp", 1), "replica")


def local(ends_in, live, gain_attn, w_qkv, w_out, gain_mlp, w_up, w_down):
    me = lax.axis_index("section")
    first = me == 0
    shards = lax.axis_size("fsdp")
    slots, length, width = ends_in.shape[1:]
    share = slots // 2
    rows = -(-length // 16) * 16
    depth = w_qkv.shape[1]
    ratio = w_up.shape[2] // width

    def columns(matrix):
        return matrix[0].reshape(depth, -1, width).transpose(1, 0, 2)

    attn_own = jnp.concatenate([columns(w_qkv), columns(w_out)]).reshape(2, 2, depth, width)
    mlp_own = jnp.stack([columns(w_up), w_down[0].reshape(ratio, depth, width)])
    gains_own = jnp.stack([gain_attn[0], gain_mlp[0]])

    def by_layer(own):
        kept, came = pick(own, me), swap_section(pick(own, 1 - me))
        return jnp.where(first, kept, came), jnp.where(first, came, kept)

    attn_halves = by_layer(attn_own)
    mlp_halves = by_layer(mlp_own)
    gains_mine = spread(gains_own, "fsdp").transpose(1, 0, 2).reshape(2, 1, width).astype(F32)
    gains_other = swap_section(gains_mine.astype(BF)).astype(F32)
    gains = (jnp.where(first, gains_mine, gains_other), jnp.where(first, gains_other, gains_mine))

    images = ends_in[0].reshape(2, share, length, width)
    kept = pick(images, me)
    came = swap_section(pick(images, 1 - me))
    slot_ids = jnp.arange(slots, dtype=jnp.int32)
    per_micro = slots // live.shape[0]
    mask = (slot_ids % per_micro < live[:, 0][slot_ids // per_micro]).reshape(2, share)
    mask = pick(mask, me)[:, None, None]
    pad = ((0, 0), (0, rows - length), (0, 0))
    x0 = jnp.pad(jnp.where(first, kept, came), pad)
    cot1 = jnp.pad(jnp.where(mask, jnp.where(first, came, kept), 0), pad)

    def attn_weights(layer):
        blocks = gather_group(attn_halves[layer], me)
        return blocks[:3].transpose(1, 0, 2).reshape(width, 3 * width), blocks[3]

    def mlp_weights(layer):
        blocks = gather_group(mlp_halves[layer], me)
        up = blocks[:ratio].transpose(1, 0, 2).reshape(width, ratio * width)
        down = blocks[ratio:].reshape(ratio, shards, depth, width).transpose(1, 0, 2, 3)
        return up, down.reshape(ratio * width, width)

    weights = [attn_weights(l) + mlp_weights(l) for l in range(2)]

    def forward(x, layer):
        wqkv, wout, wup, wdown = weights[layer]
        qkv, probs, mixt, mid = attn_fwd(x, length, gains[layer][0], wqkv, wout)
        out, act, slope = mlp_fwd(mid, gains[layer][1], wup, wdown)
        return out, (x, qkv, probs, mixt, mid, act, slope)

    def backward(cot, kept, layer):
        wqkv, wout, wup, wdown = weights[layer]
        x, qkv, probs, mixt, mid, act, slope = kept
        gmid, gup, gdown = mlp_bwd(cot, mid, act, slope, gains[layer][1], wup, wdown)
        gup = gup.reshape(shards, depth, ratio, width).transpose(2, 0, 1, 3)
        gdown = gdown.reshape(shards, ratio, depth, width).transpose(1, 0, 2, 3)
        mlp_sum = reduce_group(jnp.stack([gup, gdown]), me)
        gx, gqkv, gout = attn_bwd(gmid, x, qkv, probs, mixt, gains[layer][0], wqkv, wout)
        gqkv = gqkv.reshape(shards, depth, 3, width).transpose(2, 0, 1, 3)
        gout = gout.reshape(1, shards, depth, width)
        attn_sum = reduce_group(jnp.concatenate([gqkv, gout]).reshape(2, 2, shards, depth, width), me)
        return gx, attn_sum, mlp_sum

    x1, kept0 = forward(x0, 0)
    out, kept1 = forward(x1, 1)
    cot0, attn_sum1, mlp_sum1 = backward(cot1, kept1, 1)
    gx, attn_sum0, mlp_sum0 = backward(cot0, kept0, 0)

    def own_layer(sum0, sum1):
        mine = jnp.where(first, sum0, sum1)
        other = swap_section(jnp.where(first, sum1, sum0))
        return jnp.concatenate([jnp.where(first, mine, other), jnp.where(first, other, mine)]).astype(F32)

    mlp_grad = own_layer(mlp_sum0, mlp_sum1)
    attn_grad = own_layer(attn_sum0, attn_sum1)

    def rows_of(blocks):
        return blocks.transpose(1, 0, 2).reshape(1, depth, -1)

    grad_qkv, grad_out = rows_of(attn_grad[:3]), attn_grad[3:]
    grad_up, grad_down = rows_of(mlp_grad[:ratio]), mlp_grad[ratio:].reshape(1, ratio * depth, width)
    grad_gain_attn = jnp.sum(grad_qkv * w_qkv.astype(F32), axis=-1) / gain_attn.astype(F32)
    grad_gain_mlp = jnp.sum(grad_up * w_up.astype(F32), axis=-1) / gain_mlp.astype(F32)

    gx = gx[:, :length]
    out = jnp.where(mask, out[:, :length], 0)
    came = swap_section(jnp.where(first, out, gx))
    ends_out = jnp.zeros(images.shape, BF)
    ends_out = lax.dynamic_update_index_in_dim(ends_out, jnp.where(first, gx, out), me, 0)
    ends_out = lax.dynamic_update_index_in_dim(ends_out, came, 1 - me, 0)
    return (ends_out.reshape(ends_in.shape), grad_gain_attn, grad_qkv, grad_out, grad_gain_mlp, grad_up, grad_down)


def solution(mesh):
    in_specs = (
        P("section", ("fsdp", "replica"), None, None),
        P(None, ("fsdp", "replica")),
        P("section", "fsdp"),
        P("section", "fsdp", None),
        P("section", "fsdp", None),
        P("section", "fsdp"),
        P("section", "fsdp", None),
        P("section", "fsdp", None),
    )
    out_specs = (
        P("section", ("fsdp", "replica"), None, None),
        P("section", "fsdp"),
        P("section", "fsdp", None),
        P("section", "fsdp", None),
        P("section", "fsdp"),
        P("section", "fsdp", None),
        P("section", "fsdp", None),
    )
    return jax.shard_map(local, mesh=mesh, in_specs=in_specs, out_specs=out_specs, check_vma=False)
```

time: 1050 us -> 419 us (0.40)
  waiting for transfers between devices: 414 us -> 80.2 us
  matrix products: 219 us -> 0 us
  Pallas kernels: 0 us -> 168 us
  local copies, waits for them, and re-layouts: 227 us -> 67.8 us
  other arithmetic: 107 us -> 24.2 us
  starting transfers between devices: 8.29 us -> 70.3 us
  blocking collectives: 38.5 us -> 0 us
  between operations: 15 us -> 1.98 us
    reduce_scatter x4 -> x0, waiting for transfers between devices: 252 us -> none  [local(): lax.psum_scatter(shortened(local_grads), 'fsdp', scatter_dimension=1, til...]
    dot_general x34 -> x0, matrix products: 196 us -> none  [the longest x8 49.4 us: project(): jnp.einsum('bsk,kn->bsn', left_side, right_side, preferred_element_type=j...]
    pallas_call x0 -> x8, Pallas kernels: none -> 168 us  [call(): pl.pallas_call(body, name=name, grid=(images // g,), in_specs=[per_image(...]
    cond x106 -> x0, local copies, waits for them, and re-layouts: 107 us -> none
    another operation x31 -> x11, local copies, waits for them, and re-layouts: 71.2 us -> 3.28 us
    ppermute x4 -> x54, starting transfers between devices: 7.93 us -> 70.3 us  [the longest x15 31.2 us: swap_section(): return lax.ppermute(value, 'section', [(0, 1), (1, 0)])]
    convert_element_type x27 -> x10, other arithmetic: 61.4 us -> 7.79 us  [the longest x4 5.09 us: reduce_group(): chip = (pick(halves, me).astype(F32) + other.astype(F32)).astype(BF)]
    unnamed x11 -> x0, waiting for transfers between devices: 50.2 us -> none
  transfers between devices with their start and end apart: 13 -> 54, of which waited for: 10 -> 22; matrix products, arithmetic and copies ran while one was open for 25% -> 17% of each run, Pallas kernels for 0% -> 17%
where the time goes in v1:
time: 419 us; the launch traced here: 413 us
  Pallas kernels  168 us (40%)
  waiting for transfers between devices  80.2 us (19%)
  starting transfers between devices  70.3 us (17%)
  local copies, waits for them, and re-layouts  67.8 us (16%)
  other arithmetic  24.2 us (6%)
    pallas_call x8, Pallas kernels, call(): pl.pallas_call(body, name=name, grid=(images // g,), in_specs=[per_image(...  168 us
    ppermute x12, waiting for transfers between devices, all_sum(): lax.ppermute(value, axis, [(i, i ^ k) for i in range(size)]).astype(F32)  45 us
    ppermute x15, starting transfers between devices, swap_section(): return lax.ppermute(value, 'section', [(0, 1), (1, 0)])  31.2 us
    ppermute x12, waiting for transfers between devices, scatter_sum(): lax.ppermute(sent, axis, [(i, i ^ k) for i in range(size)]).astype(F32)  23 us
    ppermute x12, starting transfers between devices, all_sum(): lax.ppermute(value, axis, [(i, i ^ k) for i in range(size)]).astype(F32)  20.5 us
    ppermute x15, starting transfers between devices, spread(): piece = lax.ppermute(value, axis, [(i, i ^ k) for i in range(size)])  12 us
    ppermute x15, waiting for transfers between devices, spread(): piece = lax.ppermute(value, axis, [(i, i ^ k) for i in range(size)])  9.44 us
    unnamed x63, local copies, waits for them, and re-layouts  8.83 us
  transfers between devices with their start and end apart: 54, of which 22 were waited for; matrix products, arithmetic and copies ran while one was open for 17% of the time, Pallas kernels for 17%

profile of v1, /device:TPU:13, one launch (start us, length us, event | category | flops | bytes accessed | tf_op | source)
XLA Modules:
  0.0 413.0 jit_solution(12478395257272302695)
XLA Ops:
  31.8 5.3 %collective-permute-start.9 = (bf16[4,2,96,384]{3,2,0,1:T(8,128)(2,1)S(1)}, bf16[4,2,96,384]{3,2,0,1:T(8,128)(2,1)S(1)}, u32[]{:S(2)}, u32[]{:S(2)}) collective-permute-start(bf16[4,2,96,384]{3,2,0,1:T(8,128)(2,1)S(1)} %bitcast_dynamic-update-slice_fusion.22), channel_id=1, source_target_pairs={{0,16},{16,0},{1,17},{17,1},{2,18},{18,2},{3,19},{19,3},{4,20},{20... | collective-permute-start | bytes 1769480 | tf_op jit(solution)/shard_map/ppermute | solution.py:266
  37.8 3.5 collective-permute-start.18
  50.5 7.7 %collective-permute-start.14 = (bf16[4,4,96,384]{3,2,0,1:T(8,128)(2,1)}, bf16[4,4,96,384]{3,2,0,1:T(8,128)(2,1)}, u32[]{:S(2)}, u32[]{:S(2)}) collective-permute-start(bf16[4,4,96,384]{3,2,0,1:T(8,128)(2,1)} %bitcast_dynamic-update-slice_fusion.17), channel_id=1, source_target_pairs={{0,16},{16,0},{1,17},{17,1},{2,18},{18,2},{3,19},{19,3},{4,20},{20... | collective-permute-start | bytes 3538952 | tf_op jit(solution)/shard_map/ppermute | solution.py:266
  58.2 5.4 %collective-permute-start.22 = (bf16[4,4,96,384]{3,2,0,1:T(8,128)(2,1)S(1)}, bf16[4,4,96,384]{3,2,0,1:T(8,128)(2,1)}, u32[]{:S(2)}, u32[]{:S(2)}) collective-permute-start(bf16[4,4,96,384]{3,2,0,1:T(8,128)(2,1)S(1)} %bitcast_dynamic-update-slice_fusion.10), channel_id=1, source_target_pairs={{0,16},{16,0},{1,17},{17,1},{2,18},{18,2},{3,19},{19,3},{4,20},{20... | collective-permute-start | bytes 3538952 | tf_op jit(solution)/shard_map/ppermute | solution.py:266
  88.4 20.2 %attention_forward.2 = (bf16[10,208,1152]{2,1,0:T(8,128)(2,1)}, bf16[10,6,208,208]{3,2,1,0:T(8,128)(2,1)}, bf16[10,384,208]{2,1,0:T(8,128)(2,1)}, f32[10,208,384]{2,1,0:T(8,128)}) custom-call(bf16[10,208,384]{2,1,0:T(8,128)(2,1)} %pad.8.x_ref, f32[1,384]{1,0:T(1,128)} %get-tuple-element.106.gain_ref, bf16[384,1152]{1,0:T(8,128)(2,1)} %copy.85.wqkv_ref, ...), custom_call_target="tpu_custom_call" | custom-call | flops 3118202880 | bytes 17554944 | tf_op jit(solution)/shard_map/attention_forward/pallas_call | solution.py:211
  117.8 13.4 %mlp_forward.2 = (bf16[10,208,384]{2,1,0:T(8,128)(2,1)}, bf16[10,208,1536]{2,1,0:T(8,128)(2,1)}, bf16[10,208,1536]{2,1,0:T(8,128)(2,1)}) custom-call(f32[10,208,384]{2,1,0:T(8,128)} %get-tuple-element.33.mid_ref, f32[1,384]{1,0:T(1,128)} %get-tuple-element.105.gain_ref, bf16[384,1536]{1,0:T(8,128)(2,1)} %bitcast.304, bf16[1536,384]{1,0:T(8,128)(2,1)} %bitcast.306), custom_call_target="tpu_custom_call" | custom-call | flops 4907335680 | bytes 19932672 | tf_op jit(solution)/shard_map/mlp_forward/pallas_call | solution.py:211
  131.2 20.3 %attention_forward.3 = (bf16[10,208,1152]{2,1,0:T(8,128)(2,1)}, bf16[10,6,208,208]{3,2,1,0:T(8,128)(2,1)}, bf16[10,384,208]{2,1,0:T(8,128)(2,1)}, f32[10,208,384]{2,1,0:T(8,128)}) custom-call(bf16[10,208,384]{2,1,0:T(8,128)(2,1)} %get-tuple-element.34.x_ref, f32[1,384]{1,0:T(1,128)} %get-tuple-element.102.gain_ref, bf16[384,1152]{1,0:T(8,128)(2,1)} %copy.97.wqkv_ref, ...), custom_call_target="tpu_custom_call" | custom-call | flops 3118202880 | bytes 17554944 | tf_op jit(solution)/shard_map/attention_forward/pallas_call | solution.py:211
  151.5 13.6 %mlp_forward.3 = (bf16[10,208,384]{2,1,0:T(8,128)(2,1)}, bf16[10,208,1536]{2,1,0:T(8,128)(2,1)}, bf16[10,208,1536]{2,1,0:T(8,128)(2,1)}) custom-call(f32[10,208,384]{2,1,0:T(8,128)} %get-tuple-element.35.mid_ref, f32[1,384]{1,0:T(1,128)} %get-tuple-element.101.gain_ref, bf16[384,1536]{1,0:T(8,128)(2,1)} %bitcast.308, bf16[1536,384]{1,0:T(8,128)(2,1)} %bitcast.310), custom_call_target="tpu_custom_call" | custom-call | flops 4907335680 | bytes 19932672 | tf_op jit(solution)/shard_map/mlp_forward/pallas_call | solution.py:211
  165.1 21.0 %mlp_backward.2 = (f32[10,208,384]{2,1,0:T(8,128)}, bf16[384,1536]{1,0:T(8,128)(2,1)}, bf16[1536,384]{1,0:T(8,128)(2,1)}) custom-call(bf16[10,208,384]{2,1,0:T(8,128)(2,1)} %pad.7.cot_ref, f32[10,208,384]{2,1,0:T(8,128)} %get-tuple-element.35.mid_ref, bf16[10,208,1536]{2,1,0:T(8,128)(2,1)} %get-tuple-element.36.act_ref, ...), custom_call_target="tpu_custom_call" | custom-call | flops 9814671360 | bytes 25486848 | tf_op jit(solution)/shard_map/mlp_backward/pallas_call | solution.py:211
  186.1 29.4 %attention_backward.2 = (bf16[10,208,384]{2,1,0:T(8,128)(2,1)}, bf16[384,1152]{1,0:T(8,128)(2,1)}, bf16[384,384]{1,0:T(8,128)(2,1)}) custom-call(f32[10,208,384]{2,1,0:T(8,128)} %get-tuple-element.38.gmid_ref, bf16[10,208,384]{2,1,0:T(8,128)(2,1)} %get-tuple-element.34.x_ref, bf16[10,208,1152]{2,1,0:T(8,128)(2,1)} %get-tuple-element.39.qkv_ref, ...), custom_call_target="tpu_custom_call" | custom-call | flops 6568673280 | bytes 20332032 | tf_op jit(solution)/shard_map/attention_backward/pallas_call | solution.py:211
  221.4 21.2 %mlp_backward.3 = (f32[10,208,384]{2,1,0:T(8,128)}, bf16[384,1536]{1,0:T(8,128)(2,1)}, bf16[1536,384]{1,0:T(8,128)(2,1)}) custom-call(bf16[10,208,384]{2,1,0:T(8,128)(2,1)} %get-tuple-element.42.cot_ref, f32[10,208,384]{2,1,0:T(8,128)} %get-tuple-element.33.mid_ref, bf16[10,208,1536]{2,1,0:T(8,128)(2,1)} %get-tuple-element.43.act_ref, ...), custom_call_target="tpu_custom_call" | custom-call | flops 9814671360 | bytes 25486848 | tf_op jit(solution)/shard_map/mlp_backward/pallas_call | solution.py:211
  242.5 29.4 %attention_backward.3 = (bf16[10,208,384]{2,1,0:T(8,128)(2,1)}, bf16[384,1152]{1,0:T(8,128)(2,1)}, bf16[384,384]{1,0:T(8,128)(2,1)}) custom-call(f32[10,208,384]{2,1,0:T(8,128)} %get-tuple-element.45.gmid_ref, bf16[10,208,384]{2,1,0:T(8,128)(2,1)} %pad.8.x_ref, bf16[10,208,1152]{2,1,0:T(8,128)(2,1)} %get-tuple-element.46.qkv_ref, ...), custom_call_target="tpu_custom_call" | custom-call | flops 6568673280 | bytes 20332032 | tf_op jit(solution)/shard_map/attention_backward/pallas_call | solution.py:211
  288.1 3.1 collective-permute-done.33
  299.5 7.3 %collective-permute-done.36 = bf16[2,96,384]{2,1,0:T(8,128)(2,1)S(1)} collective-permute-done((bf16[2,96,384]{2,1,0:T(8,128)(2,1)S(1)}, bf16[2,96,384]{2,1,0:T(8,128)(2,1)S(1)}, u32[]{:S(2)}, u32[]{:S(2)}) %collective-permute-start.36) | collective-permute-done | bytes 147488 | tf_op jit(solution)/shard_map/ppermute | solution.py:308
  308.3 3.2 reshape.198
  314.3 3.5 collective-permute-start.39
  319.0 3.2 collective-permute-done.30
  335.6 3.3 collective-permute-done.47
  340.4 4.4 %collective-permute-done.49 = bf16[4,96,384]{2,1,0:T(8,128)(2,1)} collective-permute-done((bf16[4,96,384]{2,1,0:T(8,128)(2,1)}, bf16[4,96,384]{2,1,0:T(8,128)(2,1)}, u32[]{:S(2)}, u32[]{:S(2)}) %collective-permute-start.49) | collective-permute-done | bytes 294944 | tf_op jit(solution)/shard_map/ppermute | solution.py:298
  346.1 5.5 %collective-permute-done.40 = bf16[4,96,384]{2,1,0:T(8,128)(2,1)} collective-permute-done((bf16[4,96,384]{2,1,0:T(8,128)(2,1)}, bf16[4,96,384]{2,1,0:T(8,128)(2,1)}, u32[]{:S(2)}, u32[]{:S(2)}) %collective-permute-start.40) | collective-permute-done | bytes 294944 | tf_op jit(solution)/shard_map/ppermute | solution.py:298
  354.1 6.2 %collective-permute-start.52 = (bf16[4,96,384]{2,1,0:T(8,128)(2,1)S(1)}, bf16[4,96,384]{2,1,0:T(8,128)(2,1)S(1)}, u32[]{:S(2)}, u32[]{:S(2)}) collective-permute-start(bf16[4,96,384]{2,1,0:T(8,128)(2,1)S(1)} %fusion.15), channel_id=1, source_target_pairs={{0,3},{1,2},{2,1},{3,0},{4,7},{5,6},{6,5},{7,4},{8,11},{9,10},{10,... | collective-permute-start | bytes 884744 | tf_op jit(solution)/shard_map/ppermute | solution.py:308
  362.7 7.8 %collective-permute-start.45 = (bf16[4,96,384]{2,1,0:T(8,128)(2,1)S(1)}, bf16[4,96,384]{2,1,0:T(8,128)(2,1)S(1)}, u32[]{:S(2)}, u32[]{:S(2)}) collective-permute-start(bf16[4,96,384]{2,1,0:T(8,128)(2,1)S(1)} %fusion.18), channel_id=1, source_target_pairs={{0,3},{1,2},{2,1},{3,0},{4,7},{5,6},{6,5},{7,4},{8,11},{9,10},{10,... | collective-permute-start | bytes 884744 | tf_op jit(solution)/shard_map/ppermute | solution.py:308
  371.7 20.0 %collective-permute-done.52 = bf16[4,96,384]{2,1,0:T(8,128)(2,1)S(1)} collective-permute-done((bf16[4,96,384]{2,1,0:T(8,128)(2,1)S(1)}, bf16[4,96,384]{2,1,0:T(8,128)(2,1)S(1)}, u32[]{:S(2)}, u32[]{:S(2)}) %collective-permute-start.52) | collective-permute-done | bytes 294944 | tf_op jit(solution)/shard_map/ppermute | solution.py:308
  393.3 11.0 %collective-permute-done.45 = bf16[4,96,384]{2,1,0:T(8,128)(2,1)S(1)} collective-permute-done((bf16[4,96,384]{2,1,0:T(8,128)(2,1)S(1)}, bf16[4,96,384]{2,1,0:T(8,128)(2,1)S(1)}, u32[]{:S(2)}, u32[]{:S(2)}) %collective-permute-start.45) | collective-permute-done | bytes 294944 | tf_op jit(solution)/shard_map/ppermute | solution.py:308
  (282 shorter events, 142.3 us)
Async XLA Ops:
  5.4 15.1 %collective-permute-start.10 = (bf16[4,96,384]{2,1,0:T(8,128)(2,1)S(1)}, bf16[4,96,384]{2,1,0:T(8,128)(2,1)S(1)}, u32[]{:S(2)}, u32[]{:S(2)}) collective-permute-start(bf16[4,96,384]{2,1,0:T(8,128)(2,1)S(1)} %fusion.20), channel_id=1, source_target_pairs={{0,16},{16,0},{1,17},{17,1},{2,18},{18,2},{3,19},{19,3},{4,20},{20... | collective-permute-start | bytes 884744 | tf_op jit(solution)/shard_map/ppermute | solution.py:266
  12.8 70.7 %collective-permute-start = (bf16[10,197,384]{2,1,0:T(8,128)(2,1)}, bf16[10,197,384]{2,1,0:T(8,128)(2,1)}, u32[]{:S(2)}, u32[]{:S(2)}) collective-permute-start(bf16[10,197,384]{2,1,0:T(8,128)(2,1)} %dynamic-slice_bitcast_fusion), channel_id=1, source_target_pairs={{0,16},{16,0},{1,17},{17,1},{2,18},{18,2},{3,19},{19,3},{4,20},{20... | collective-permute-start | bytes 4538888 | tf_op jit(solution)/shard_map/ppermute | solution.py:266
  29.2 13.3 %collective-permute-start.12 = (bf16[4,96,384]{2,1,0:T(8,128)(2,1)S(1)}, bf16[4,96,384]{2,1,0:T(8,128)(2,1)S(1)}, u32[]{:S(2)}, u32[]{:S(2)}) collective-permute-start(bf16[4,96,384]{2,1,0:T(8,128)(2,1)S(1)} %get-tuple-element.70), channel_id=1, source_target_pairs={{0,8},{4,12},{8,0},{12,4},{1,9},{5,13},{9,1},{13,5},{2,10},{6,14},... | collective-permute-start | bytes 884744 | tf_op jit(solution)/shard_map/ppermute | solution.py:285
  31.8 34.3 %collective-permute-start.9 = (bf16[4,2,96,384]{3,2,0,1:T(8,128)(2,1)S(1)}, bf16[4,2,96,384]{3,2,0,1:T(8,128)(2,1)S(1)}, u32[]{:S(2)}, u32[]{:S(2)}) collective-permute-start(bf16[4,2,96,384]{3,2,0,1:T(8,128)(2,1)S(1)} %bitcast_dynamic-update-slice_fusion.22), channel_id=1, source_target_pairs={{0,16},{16,0},{1,17},{17,1},{2,18},{18,2},{3,19},{19,3},{4,20},{20... | collective-permute-start | bytes 1769480 | tf_op jit(solution)/shard_map/ppermute | solution.py:266
  37.8 28.2 %collective-permute-start.18 = (bf16[4,2,96,384]{3,2,0,1:T(8,128)(2,1)S(1)}, bf16[4,2,96,384]{3,2,0,1:T(8,128)(2,1)S(1)}, u32[]{:S(2)}, u32[]{:S(2)}) collective-permute-start(bf16[4,2,96,384]{3,2,0,1:T(8,128)(2,1)S(1)} %bitcast_dynamic-update-slice_fusion.18), channel_id=1, source_target_pairs={{0,16},{16,0},{1,17},{17,1},{2,18},{18,2},{3,19},{19,3},{4,20},{20... | collective-permute-start | bytes 1769480 | tf_op jit(solution)/shard_map/ppermute | solution.py:266
  50.5 58.1 %collective-permute-start.14 = (bf16[4,4,96,384]{3,2,0,1:T(8,128)(2,1)}, bf16[4,4,96,384]{3,2,0,1:T(8,128)(2,1)}, u32[]{:S(2)}, u32[]{:S(2)}) collective-permute-start(bf16[4,4,96,384]{3,2,0,1:T(8,128)(2,1)} %bitcast_dynamic-update-slice_fusion.17), channel_id=1, source_target_pairs={{0,16},{16,0},{1,17},{17,1},{2,18},{18,2},{3,19},{19,3},{4,20},{20... | collective-permute-start | bytes 3538952 | tf_op jit(solution)/shard_map/ppermute | solution.py:266
  58.2 54.5 %collective-permute-start.22 = (bf16[4,4,96,384]{3,2,0,1:T(8,128)(2,1)S(1)}, bf16[4,4,96,384]{3,2,0,1:T(8,128)(2,1)}, u32[]{:S(2)}, u32[]{:S(2)}) collective-permute-start(bf16[4,4,96,384]{3,2,0,1:T(8,128)(2,1)S(1)} %bitcast_dynamic-update-slice_fusion.10), channel_id=1, source_target_pairs={{0,16},{16,0},{1,17},{17,1},{2,18},{18,2},{3,19},{19,3},{4,20},{20... | collective-permute-start | bytes 3538952 | tf_op jit(solution)/shard_map/ppermute | solution.py:266
  221.4 59.9 %collective-permute-start.31 = (bf16[2,4,96,384]{3,2,0,1:T(8,128)(2,1)}, bf16[2,4,96,384]{3,2,0,1:T(8,128)(2,1)}, u32[]{:S(2)}, u32[]{:S(2)}) collective-permute-start(bf16[2,4,96,384]{3,2,0,1:T(8,128)(2,1)} %bitcast.269), channel_id=1, source_target_pairs={{0,16},{16,0},{1,17},{17,1},{2,18},{18,2},{3,19},{19,3},{4,20},{20... | collective-permute-start | bytes 1769480 | tf_op jit(solution)/shard_map/ppermute | solution.py:266
  280.8 45.0 %collective-permute-start.46 = (bf16[4,4,96,384]{3,2,0,1:T(8,128)(2,1)}, bf16[4,4,96,384]{3,2,0,1:T(8,128)(2,1)}, u32[]{:S(2)}, u32[]{:S(2)}) collective-permute-start(bf16[4,4,96,384]{3,2,0,1:T(8,128)(2,1)} %fusion.4), channel_id=1, source_target_pairs={{0,16},{16,0},{1,17},{17,1},{2,18},{18,2},{3,19},{19,3},{4,20},{20... | collective-permute-start | bytes 3538952 | tf_op jit(solution)/shard_map/ppermute | solution.py:266
  296.7 17.6 %collective-permute-start.37 = (bf16[2,96,384]{2,1,0:T(8,128)(2,1)S(1)}, bf16[2,96,384]{2,1,0:T(8,128)(2,1)S(1)}, u32[]{:S(2)}, u32[]{:S(2)}) collective-permute-start(bf16[2,96,384]{2,1,0:T(8,128)(2,1)S(1)} %fusion.25), channel_id=1, source_target_pairs={{0,3},{1,2},{2,1},{3,0},{4,7},{5,6},{6,5},{7,4},{8,11},{9,10},{10,... | collective-permute-start | bytes 442376 | tf_op jit(solution)/shard_map/ppermute | solution.py:308
  296.8 21.0 %collective-permute-start.28 = (bf16[2,96,384]{2,1,0:T(8,128)(2,1)S(1)}, bf16[2,96,384]{2,1,0:T(8,128)(2,1)}, u32[]{:S(2)}, u32[]{:S(2)}) collective-permute-start(bf16[2,96,384]{2,1,0:T(8,128)(2,1)S(1)} %fusion.28), channel_id=1, source_target_pairs={{0,1},{1,0},{2,3},{3,2},{4,5},{5,4},{6,7},{7,6},{8,9},{9,8},{10,11... | collective-permute-start | bytes 442376 | tf_op jit(solution)/shard_map/ppermute | solution.py:308
  298.1 20.9 %collective-permute-start.29 = (bf16[2,96,384]{2,1,0:T(8,128)(2,1)S(1)}, bf16[2,96,384]{2,1,0:T(8,128)(2,1)}, u32[]{:S(2)}, u32[]{:S(2)}) collective-permute-start(bf16[2,96,384]{2,1,0:T(8,128)(2,1)S(1)} %fusion.28), channel_id=1, source_target_pairs={{0,2},{1,3},{2,0},{3,1},{4,6},{5,7},{6,4},{7,5},{8,10},{9,11},{10,... | collective-permute-start | bytes 442376 | tf_op jit(solution)/shard_map/ppermute | solution.py:308
  306.8 15.4 %collective-permute-start.30 = (bf16[2,96,384]{2,1,0:T(8,128)(2,1)S(1)}, bf16[2,96,384]{2,1,0:T(8,128)(2,1)}, u32[]{:S(2)}, u32[]{:S(2)}) collective-permute-start(bf16[2,96,384]{2,1,0:T(8,128)(2,1)S(1)} %fusion.28), channel_id=1, source_target_pairs={{0,3},{1,2},{2,1},{3,0},{4,7},{5,6},{6,5},{7,4},{8,11},{9,10},{10,... | collective-permute-start | bytes 442376 | tf_op jit(solution)/shard_map/ppermute | solution.py:308
  314.3 19.1 %collective-permute-start.39 = (bf16[4,4,96,384]{3,2,0,1:T(8,128)(2,1)S(1)}, bf16[4,4,96,384]{3,2,0,1:T(8,128)(2,1)S(1)}, u32[]{:S(2)}, u32[]{:S(2)}) collective-permute-start(bf16[4,4,96,384]{3,2,0,1:T(8,128)(2,1)S(1)} %fusion.8), channel_id=1, source_target_pairs={{0,16},{16,0},{1,17},{17,1},{2,18},{18,2},{3,19},{19,3},{4,20},{20... | collective-permute-start | bytes 3538952 | tf_op jit(solution)/shard_map/ppermute | solution.py:266
  317.8 88.7 %collective-permute-start.23 = (bf16[10,197,384]{2,1,0:T(8,128)(2,1)}, bf16[10,197,384]{2,1,0:T(8,128)(2,1)}, u32[]{:S(2)}, u32[]{:S(2)}) collective-permute-start(bf16[10,197,384]{2,1,0:T(8,128)(2,1)} %broadcast_select_fusion), channel_id=1, source_target_pairs={{0,16},{16,0},{1,17},{17,1},{2,18},{18,2},{3,19},{19,3},{4,20},{20... | collective-permute-start | bytes 4538888 | tf_op jit(solution)/shard_map/ppermute | solution.py:266
  331.3 13.4 %collective-permute-start.49 = (bf16[4,96,384]{2,1,0:T(8,128)(2,1)}, bf16[4,96,384]{2,1,0:T(8,128)(2,1)}, u32[]{:S(2)}, u32[]{:S(2)}) collective-permute-start(bf16[4,96,384]{2,1,0:T(8,128)(2,1)} %get-tuple-element.82), channel_id=1, source_target_pairs={{0,12},{4,8},{8,4},{12,0},{1,13},{5,9},{9,5},{13,1},{2,14},{6,10},... | collective-permute-start | bytes 884744 | tf_op jit(solution)/shard_map/ppermute | solution.py:298
  335.0 16.6 %collective-permute-start.40 = (bf16[4,96,384]{2,1,0:T(8,128)(2,1)}, bf16[4,96,384]{2,1,0:T(8,128)(2,1)}, u32[]{:S(2)}, u32[]{:S(2)}) collective-permute-start(bf16[4,96,384]{2,1,0:T(8,128)(2,1)} %get-tuple-element.84), channel_id=1, source_target_pairs={{0,4},{4,0},{8,12},{12,8},{1,5},{5,1},{9,13},{13,9},{2,6},{6,2},{1... | collective-permute-start | bytes 884744 | tf_op jit(solution)/shard_map/ppermute | solution.py:298
  338.9 15.2 %collective-permute-start.41 = (bf16[4,96,384]{2,1,0:T(8,128)(2,1)}, bf16[4,96,384]{2,1,0:T(8,128)(2,1)S(1)}, u32[]{:S(2)}, u32[]{:S(2)}) collective-permute-start(bf16[4,96,384]{2,1,0:T(8,128)(2,1)} %get-tuple-element.86), channel_id=1, source_target_pairs={{0,8},{4,12},{8,0},{12,4},{1,9},{5,13},{9,1},{13,5},{2,10},{6,14},... | collective-permute-start | bytes 884744 | tf_op jit(solution)/shard_map/ppermute | solution.py:298
  339.3 21.0 %collective-permute-start.42 = (bf16[4,96,384]{2,1,0:T(8,128)(2,1)}, bf16[4,96,384]{2,1,0:T(8,128)(2,1)S(1)}, u32[]{:S(2)}, u32[]{:S(2)}) collective-permute-start(bf16[4,96,384]{2,1,0:T(8,128)(2,1)} %get-tuple-element.85), channel_id=1, source_target_pairs={{0,12},{4,8},{8,4},{12,0},{1,13},{5,9},{9,5},{13,1},{2,14},{6,10},... | collective-permute-start | bytes 884744 | tf_op jit(solution)/shard_map/ppermute | solution.py:298
  346.1 15.4 %collective-permute-start.50 = (bf16[4,96,384]{2,1,0:T(8,128)(2,1)S(1)}, bf16[4,96,384]{2,1,0:T(8,128)(2,1)S(1)}, u32[]{:S(2)}, u32[]{:S(2)}) collective-permute-start(bf16[4,96,384]{2,1,0:T(8,128)(2,1)S(1)} %fusion.15), channel_id=1, source_target_pairs={{0,1},{1,0},{2,3},{3,2},{4,5},{5,4},{6,7},{7,6},{8,9},{9,8},{10,11... | collective-permute-start | bytes 884744 | tf_op jit(solution)/shard_map/ppermute | solution.py:308
  354.1 37.6 %collective-permute-start.52 = (bf16[4,96,384]{2,1,0:T(8,128)(2,1)S(1)}, bf16[4,96,384]{2,1,0:T(8,128)(2,1)S(1)}, u32[]{:S(2)}, u32[]{:S(2)}) collective-permute-start(bf16[4,96,384]{2,1,0:T(8,128)(2,1)S(1)} %fusion.15), channel_id=1, source_target_pairs={{0,3},{1,2},{2,1},{3,0},{4,7},{5,6},{6,5},{7,4},{8,11},{9,10},{10,... | collective-permute-start | bytes 884744 | tf_op jit(solution)/shard_map/ppermute | solution.py:308
  361.4 30.3 %collective-permute-start.43 = (bf16[4,96,384]{2,1,0:T(8,128)(2,1)S(1)}, bf16[4,96,384]{2,1,0:T(8,128)(2,1)S(1)}, u32[]{:S(2)}, u32[]{:S(2)}) collective-permute-start(bf16[4,96,384]{2,1,0:T(8,128)(2,1)S(1)} %fusion.18), channel_id=1, source_target_pairs={{0,1},{1,0},{2,3},{3,2},{4,5},{5,4},{6,7},{7,6},{8,9},{9,8},{10,11... | collective-permute-start | bytes 884744 | tf_op jit(solution)/shard_map/ppermute | solution.py:308
  361.5 31.8 %collective-permute-start.44 = (bf16[4,96,384]{2,1,0:T(8,128)(2,1)S(1)}, bf16[4,96,384]{2,1,0:T(8,128)(2,1)S(1)}, u32[]{:S(2)}, u32[]{:S(2)}) collective-permute-start(bf16[4,96,384]{2,1,0:T(8,128)(2,1)S(1)} %fusion.18), channel_id=1, source_target_pairs={{0,2},{1,3},{2,0},{3,1},{4,6},{5,7},{6,4},{7,5},{8,10},{9,11},{10,... | collective-permute-start | bytes 884744 | tf_op jit(solution)/shard_map/ppermute | solution.py:308
  362.7 41.6 %collective-permute-start.45 = (bf16[4,96,384]{2,1,0:T(8,128)(2,1)S(1)}, bf16[4,96,384]{2,1,0:T(8,128)(2,1)S(1)}, u32[]{:S(2)}, u32[]{:S(2)}) collective-permute-start(bf16[4,96,384]{2,1,0:T(8,128)(2,1)S(1)} %fusion.18), channel_id=1, source_target_pairs={{0,3},{1,2},{2,1},{3,0},{4,7},{5,6},{6,5},{7,4},{8,11},{9,10},{10,... | collective-permute-start | bytes 884744 | tf_op jit(solution)/shard_map/ppermute | solution.py:308
  (61 other events, 459.8 us)

commit v2 on v1

v2 whole, which is shorter than its diff:
```python
import functools

import jax
import jax.numpy as jnp
from jax import lax
from jax.experimental import pallas as pl
from jax.experimental.pallas import tpu as pltpu
from jax.sharding import PartitionSpec as P

HEADS = 6
HEAD_DIM = 64
PAIR = 2 * HEAD_DIM
EPS = 1e-06
BF = jnp.bfloat16
F32 = jnp.float32
VMEM_LIMIT = 56 * 1024 * 1024
PER_STEP = 2
MOST_PIECES = 8


def dot_nn(a, b):
    return lax.dot_general(a, b, (((1,), (0,)), ((), ())), preferred_element_type=F32)


def dot_nt(a, b):
    return lax.dot_general(a, b, (((1,), (1,)), ((), ())), preferred_element_type=F32)


def norm_rows(values):
    centered = values - jnp.mean(values, axis=-1, keepdims=True)
    scale = lax.rsqrt(jnp.mean(centered * centered, axis=-1, keepdims=True) + EPS)
    return centered * scale, scale


def norm_rows_back(grad_normed, normed, scale):
    first = jnp.mean(grad_normed, axis=-1, keepdims=True)
    second = jnp.mean(grad_normed * normed, axis=-1, keepdims=True)
    return scale * (grad_normed - first - normed * second)


def gelu_both(v):
    cdf = 0.5 * (1.0 + lax.erf(v * 0.7071067811865476))
    density = jnp.exp(-0.5 * v * v) * 0.3989422804014327
    return v * cdf, cdf + v * density


def place_attn(ids_ref, pieces, weight_ref):
    count = len(pieces) // 2
    width = weight_ref.shape[0]
    depth = width // count
    for section in range(2):
        @pl.when(ids_ref[0] == section)
        def _():
            for k in range(count):
                at = pl.ds(pl.multiple_of((ids_ref[1] ^ k) * depth, depth), depth)
                for half, piece in ((section, pieces[k]), (1 - section, pieces[count + k])):
                    for b in range(2):
                        lanes = (2 * half + b) * width
                        weight_ref[at, lanes:lanes + width] = piece[b * depth:(b + 1) * depth, :]


def place_mlp(ids_ref, pieces, up_ref, down_ref):
    count = len(pieces) // 2
    width, hidden = up_ref.shape
    depth = width // count
    tall = hidden // count
    for section in range(2):
        @pl.when(ids_ref[0] == section)
        def _():
            for k in range(count):
                shard = ids_ref[1] ^ k
                at = pl.ds(pl.multiple_of(shard * depth, depth), depth)
                for half, piece in ((section, pieces[k]), (1 - section, pieces[count + k])):
                    if half == 0:
                        for b in range(hidden // width):
                            up_ref[at, b * width:(b + 1) * width] = piece[b * depth:(b + 1) * depth, :]
                    else:
                        down_ref[pl.ds(pl.multiple_of(shard * tall, tall), tall), :] = piece[...]


def attn_fwd_kernel(length, count, entering, ids_ref, *refs):
    if entering:
        own_ref, came_ref = refs[:2]
        pieces, refs = refs[2:2 + 2 * count], refs[2 + 2 * count:]
        qkv_ref, probs_ref, mixt_ref, mid_ref, weight_ref, x_ref, entry_s, qkv_s, mixed_s, pad_s = refs
    else:
        x_ref = refs[0]
        pieces, refs = refs[1:1 + 2 * count], refs[1 + 2 * count:]
        qkv_ref, probs_ref, mixt_ref, mid_ref, weight_ref, entry_s, qkv_s, mixed_s = refs
    images, rows, width = x_ref.shape

    @pl.when(pl.program_id(0) == 0)
    def _():
        place_attn(ids_ref, pieces, weight_ref)
        if entering:
            pad_s[...] = jnp.zeros_like(pad_s)

    for g in range(images):
        if entering:
            pad_s[g, :length, :] = jnp.where(ids_ref[0] == 0, own_ref[g].astype(F32), came_ref[g].astype(F32))
            values = pad_s[g]
            x_ref[g] = values.astype(BF)
        else:
            values = x_ref[g].astype(F32)
        normed, _ = norm_rows(values)
        entry_s[g * rows:(g + 1) * rows, :] = normed.astype(BF)
    qkv_s[...] = dot_nn(entry_s[...], weight_ref[:, :3 * width]).astype(BF)
    lane = lax.broadcasted_iota(jnp.int32, (rows, PAIR), 1)
    cut = (length // 8) * 8
    tail_row = lax.broadcasted_iota(jnp.int32, (rows - cut, rows), 0) + cut
    for g in range(images):
        qkv_ref[g] = qkv_s[g * rows:(g + 1) * rows, :]
        for pair in range(HEADS // 2):
            at = pair * PAIR
            q = qkv_s[g * rows:(g + 1) * rows, at:at + PAIR] * 0.125
            k = qkv_s[g * rows:(g + 1) * rows, width + at:width + at + PAIR]
            v = qkv_s[g * rows:(g + 1) * rows, 2 * width + at:2 * width + at + PAIR]
            v_t = v.T
            for side in range(2):
                own = (lane // HEAD_DIM) == side
                scores = dot_nt(k, jnp.where(own, q, jnp.zeros_like(q)))
                tail = jnp.where(tail_row < length, scores[cut:], -1e30)
                top = jnp.maximum(jnp.max(scores[:cut], axis=0, keepdims=True),
                                  jnp.max(tail, axis=0, keepdims=True))
                e_top = jnp.exp(scores[:cut] - top)
                e_tail = jnp.exp(tail - top)
                total = jnp.sum(e_top, axis=0, keepdims=True) + jnp.sum(e_tail, axis=0, keepdims=True)
                inv = 1.0 / total
                head = pair * 2 + side
                probs = jnp.concatenate([e_top * inv, e_tail * inv], axis=0).astype(BF)
                probs_ref[g, head] = probs
                mixed = dot_nn(v_t[side * HEAD_DIM:(side + 1) * HEAD_DIM], probs)
                mixt_ref[g, head * HEAD_DIM:(head + 1) * HEAD_DIM, :] = mixed.astype(BF)
        mixed_s[g * rows:(g + 1) * rows, :] = mixt_ref[g].T
    added = dot_nn(mixed_s[...], weight_ref[:, 3 * width:])
    for g in range(images):
        mid_ref[g] = x_ref[g].astype(F32) + added[g * rows:(g + 1) * rows]


def mlp_fwd_kernel(length, count, leaving, ids_ref, mid_ref, *refs):
    pieces, refs = refs[:2 * count], refs[2 * count:]
    out_ref, act_ref, slope_ref, up_ref, down_ref, entry_s, act_s = refs
    images, rows, width = mid_ref.shape
    hidden_width = up_ref.shape[1]

    @pl.when(pl.program_id(0) == 0)
    def _():
        place_mlp(ids_ref, pieces, up_ref, down_ref)

    for g in range(images):
        normed, _ = norm_rows(mid_ref[g])
        entry_s[g * rows:(g + 1) * rows, :] = normed.astype(BF)
    step = 256
    for at in range(0, hidden_width, step):
        hidden = dot_nn(entry_s[...], up_ref[:, at:at + step])
        act, slope = gelu_both(hidden)
        act_s[:, at:at + step] = act.astype(BF)
        for g in range(images):
            slope_ref[g, :, at:at + step] = slope[g * rows:(g + 1) * rows].astype(BF)
    added = dot_nn(act_s[...], down_ref[...])
    for g in range(images):
        act_ref[g] = act_s[g * rows:(g + 1) * rows, :]
        out = mid_ref[g] + added[g * rows:(g + 1) * rows]
        if leaving:
            live = pl.program_id(0) * images + g < ids_ref[2]
            out_ref[g] = jnp.where(live, out[:length], 0.0).astype(BF)
        else:
            out_ref[g] = out.astype(BF)


def mlp_bwd_kernel(length, count, entering, ids_ref, *refs):
    if entering:
        own_ref, came_ref, *refs = refs
        *refs, pad_s = refs
    else:
        cot_ref, *refs = refs
    mid_ref, act_ref, slope_ref, up_ref, down_ref, gmid_ref, keep_ref, send_ref, *refs = refs
    up_acc, down_acc, entry_t, cot_t, gh_s = refs
    images, rows, width = mid_ref.shape
    step_id = pl.program_id(0)

    @pl.when(step_id == 0)
    def _():
        up_acc[...] = jnp.zeros_like(up_acc)
        down_acc[...] = jnp.zeros_like(down_acc)
        if entering:
            pad_s[...] = jnp.zeros_like(pad_s)

    hidden_width = up_ref.shape[1]
    step = 256
    for g in range(images):
        if entering:
            live = step_id * images + g < ids_ref[2]
            came = jnp.where(ids_ref[0] == 0, came_ref[g].astype(F32), own_ref[g].astype(F32))
            pad_s[:length, :] = jnp.where(live, came, 0.0)
            cot = pad_s[...].astype(BF)
        else:
            cot = cot_ref[g]
        normed, scale = norm_rows(mid_ref[g])
        entry_t[...] = normed.astype(BF).T
        cot_t[...] = cot.T
        for at in range(0, hidden_width, step):
            grad_act = dot_nt(cot, down_ref[at:at + step, :])
            gh_s[:, at:at + step] = (grad_act * slope_ref[g, :, at:at + step].astype(F32)).astype(BF)
        up_acc[...] += dot_nn(entry_t[...], gh_s[...])
        down_acc[...] += dot_nn(cot_t[...], act_ref[g])
        grad_entry = dot_nt(gh_s[...], up_ref[...])
        gmid_ref[g] = cot.astype(F32) + norm_rows_back(grad_entry, normed, scale)

    @pl.when(step_id == pl.num_programs(0) - 1)
    def _():
        depth = width // count
        tall = hidden_width // count
        for section in range(2):
            @pl.when(ids_ref[0] == section)
            def _():
                for k in range(count):
                    shard = ids_ref[1] ^ k
                    at = pl.ds(pl.multiple_of(shard * depth, depth), depth)
                    up_out, down_out = (keep_ref, send_ref) if section == 0 else (send_ref, keep_ref)
                    for b in range(hidden_width // width):
                        up_out[k, b * depth:(b + 1) * depth, :] = up_acc[at, b * width:(b + 1) * width].astype(BF)
                    for j in range(0, tall, 128):
                        lanes = pl.ds(pl.multiple_of(shard * tall + j, 128), 128)
                        down_out[k, j:j + 128, :] = down_acc[:, lanes].T.astype(BF)


def attn_bwd_kernel(length, count, leaving, ids_ref, gmid_ref, x_ref, qkv_ref, probs_ref, mixt_ref, weight_ref,
                    gx_ref, keep_ref, send_ref, acc, joint_s, entry_t):
    images, rows, width = x_ref.shape
    step_id = pl.program_id(0)

    @pl.when(step_id == 0)
    def _():
        acc[...] = jnp.zeros_like(acc)

    lane = lax.broadcasted_iota(jnp.int32, (rows, PAIR), 1)
    for g in range(images):
        normed, scale = norm_rows(x_ref[g].astype(F32))
        entry_t[...] = normed.astype(BF).T
        low = gmid_ref[g].astype(BF)
        acc[:, 3 * width:] += dot_nn(mixt_ref[g], low)
        grad_mixed = dot_nt(low, weight_ref[:, 3 * width:]).astype(BF)
        grad_mixed_t = dot_nt(weight_ref[:, 3 * width:], low).astype(BF)
        for pair in range(HEADS // 2):
            at = pair * PAIR
            q = qkv_ref[g, :, at:at + PAIR] * 0.125
            k = qkv_ref[g, :, width + at:width + at + PAIR]
            v = qkv_ref[g, :, 2 * width + at:2 * width + at + PAIR]
            k_t = (k * 0.125).T
            gm = grad_mixed[:, at:at + PAIR]
            grad_k = None
            grad_v = None
            grad_q_t = []
            for side in range(2):
                head = pair * 2 + side
                lo = head * HEAD_DIM
                own = (lane // HEAD_DIM) == side
                gm_own = jnp.where(own, gm, jnp.zeros_like(gm))
                q_own = jnp.where(own, q, jnp.zeros_like(q))
                probs = probs_ref[g, head]
                delta = jnp.sum(grad_mixed_t[lo:lo + HEAD_DIM].astype(F32)
                                * mixt_ref[g, lo:lo + HEAD_DIM, :].astype(F32), axis=0, keepdims=True)
                grad_probs = dot_nt(v, gm_own)
                grad_scores = (probs.astype(F32) * (grad_probs - delta)).astype(BF)
                part_v = dot_nn(probs, gm_own)
                part_k = dot_nn(grad_scores, q_own)
                grad_v = part_v if grad_v is None else grad_v + part_v
                grad_k = part_k if grad_k is None else grad_k + part_k
                grad_q_t.append(dot_nn(k_t[side * HEAD_DIM:(side + 1) * HEAD_DIM], grad_scores))
            joint_s[:, at:at + PAIR] = jnp.concatenate(grad_q_t, axis=0).astype(BF).T
            joint_s[:, width + at:width + at + PAIR] = grad_k.astype(BF)
            joint_s[:, 2 * width + at:2 * width + at + PAIR] = grad_v.astype(BF)
        acc[:, :3 * width] += dot_nn(entry_t[...], joint_s[...])
        grad_entry = dot_nt(joint_s[...], weight_ref[:, :3 * width])
        grad_x = gmid_ref[g] + norm_rows_back(grad_entry, normed, scale)
        gx_ref[g] = (grad_x[:length] if leaving else grad_x).astype(BF)

    @pl.when(step_id == pl.num_programs(0) - 1)
    def _():
        depth = width // count
        for section in range(2):
            @pl.when(ids_ref[0] == section)
            def _():
                for k in range(count):
                    at = pl.ds(pl.multiple_of((ids_ref[1] ^ k) * depth, depth), depth)
                    for half, out_ref in ((section, keep_ref), (1 - section, send_ref)):
                        for b in range(2):
                            lanes = (2 * half + b) * width
                            out_ref[k, b * depth:(b + 1) * depth, :] = acc[at, lanes:lanes + width].astype(BF)


def call(body, name, ids, images, entering, streams, fixed, stream_outs, fixed_outs, scratch, flops):
    g = PER_STEP if images % PER_STEP == 0 else 1

    def entering_spec(shape):
        return pl.BlockSpec((g,) + shape[1:], lambda i, ids: (ids[0] * (images // g) + i,) + (0,) * (len(shape) - 1))

    def per_image(shape):
        return pl.BlockSpec((g,) + shape[1:], lambda i, ids: (i,) + (0,) * (len(shape) - 1))

    def whole(shape):
        return pl.BlockSpec(shape, lambda i, ids: (0,) * len(shape))

    outs = [jax.ShapeDtypeStruct(s, d) for s, d in stream_outs + fixed_outs]
    moved = sum(a.size * a.dtype.itemsize for a in list(streams) + list(fixed) + outs)
    return pl.pallas_call(
        body,
        name=name,
        grid_spec=pltpu.PrefetchScalarGridSpec(
            num_scalar_prefetch=1,
            grid=(images // g,),
            in_specs=[entering_spec(a.shape) for a in entering] + [per_image(a.shape) for a in streams]
            + [whole(a.shape) for a in fixed],
            out_specs=[per_image(s) for s, _ in stream_outs] + [whole(s) for s, _ in fixed_outs],
            scratch_shapes=scratch(g),
        ),
        out_shape=outs,
        compiler_params=pltpu.CompilerParams(vmem_limit_bytes=VMEM_LIMIT, dimension_semantics=("arbitrary",)),
        cost_estimate=pl.CostEstimate(flops=int(flops), bytes_accessed=int(moved), transcendentals=0),
    )(ids, *entering, *streams, *fixed)


def attn_fwd(ids, x, pieces, dims, entering):
    n, rows, length, width, ff = dims
    count = len(pieces) // 2
    outs = [((n, rows, 3 * width), BF), ((n, HEADS, rows, rows), BF), ((n, width, rows), BF), ((n, rows, width), F32)]
    fixed_outs = [((width, 4 * width), BF)]
    body = functools.partial(attn_fwd_kernel, length, count, entering)

    def scratch(g):
        refs = [pltpu.VMEM((g * rows, width), BF), pltpu.VMEM((g * rows, 3 * width), BF), pltpu.VMEM((g * rows, width), BF)]
        return refs + ([pltpu.VMEM((g, rows, width), F32)] if entering else [])

    flops = 2 * n * rows * width * 4 * width + 4 * n * rows * rows * width
    if entering:
        def reordered(ids_ref, *refs):
            ins, rest = refs[:2 + 2 * count], refs[2 + 2 * count:]
            qkv, probs, mixt, mid, xp, weight, *scr = rest
            body(ids_ref, *ins, qkv, probs, mixt, mid, weight, xp, *scr)
        return call(reordered, "attention_forward", ids, n, x, [], pieces, outs + [((n, rows, width), BF)], fixed_outs,
                    scratch, flops)
    qkv, probs, mixt, mid, weight = call(body, "attention_forward", ids, n, [], [x], pieces, outs, fixed_outs, scratch, flops)
    return qkv, probs, mixt, mid, x, weight


def mlp_fwd(ids, mid, pieces, dims, leaving):
    n, rows, length, width, ff = dims
    count = len(pieces) // 2
    return call(
        functools.partial(mlp_fwd_kernel, length, count, leaving), "mlp_forward", ids, n, [], [mid], pieces,
        [((n, length if leaving else rows, width), BF), ((n, rows, ff), BF), ((n, rows, ff), BF)],
        [((width, ff), BF), ((ff, width), BF)],
        lambda g: [pltpu.VMEM((g * rows, width), BF), pltpu.VMEM((g * rows, ff), BF)],
        4 * n * rows * width * ff)


def mlp_bwd(ids, cot, mid, act, slope, up, down, dims, count, entering):
    n, rows, length, width, ff = dims
    scratch = [pltpu.VMEM((width, ff), F32), pltpu.VMEM((width, ff), F32), pltpu.VMEM((width, rows), BF),
               pltpu.VMEM((width, rows), BF), pltpu.VMEM((rows, ff), BF)]
    if entering:
        scratch.append(pltpu.VMEM((rows, width), F32))
    half = (count, ff // count, width)
    return call(
        functools.partial(mlp_bwd_kernel, length, count, entering), "mlp_backward", ids, n,
        cot if entering else [], ([] if entering else [cot]) + [mid, act, slope], [up, down],
        [((n, rows, width), F32)], [(half, BF), (half, BF)], lambda g: scratch, 8 * n * rows * width * ff)


def attn_bwd(ids, gmid, x, qkv, probs, mixt, weight, dims, count, leaving):
    n, rows, length, width, ff = dims
    half = (count, 2 * width // count, width)
    return call(
        functools.partial(attn_bwd_kernel, length, count, leaving), "attention_backward", ids, n, [],
        [gmid, x, qkv, probs, mixt], [weight],
        [((n, length if leaving else rows, width), BF)], [(half, BF), (half, BF)],
        lambda g: [pltpu.VMEM((width, 4 * width), F32), pltpu.VMEM((rows, 3 * width), BF), pltpu.VMEM((width, rows), BF)],
        4 * n * rows * width * 4 * width + 10 * n * rows * rows * width)


def swap_section(value):
    return lax.ppermute(value, "section", [(0, 1), (1, 0)])


def pick(stack, index):
    return lax.dynamic_index_in_dim(stack, index, 0, keepdims=False)


def tie(*values):
    return lax.optimization_barrier(values)


def exchange(values, axis):
    size = lax.axis_size(axis)
    return [lax.ppermute(v, axis, [(i, i ^ (k + 1)) for i in range(size)]) for k, v in enumerate(values)]


def direct(size):
    return size & (size - 1) == 0 and size <= MOST_PIECES


def total(first, others):
    result = first.astype(F32)
    for other in others:
        result = result + other.astype(F32)
    return result.astype(BF)


def local(ends_in, live, gain_attn, w_qkv, w_out, gain_mlp, w_up, w_down):
    me = lax.axis_index("section")
    mine_at = lax.axis_index("fsdp")
    first = me == 0
    shards = lax.axis_size("fsdp")
    replicas = lax.axis_size("replica")
    slots, length, width = ends_in.shape[1:]
    share = slots // 2
    rows = -(-length // 16) * 16
    depth = w_qkv.shape[1]
    ff = w_up.shape[2]
    ratio = ff // width
    dims = (share, rows, length, width, ff)
    packed = direct(shards) and depth % 16 == 0
    count = shards if packed else 1

    live_here = pick(live[:, 0], me)
    ids = jnp.stack([me, mine_at if packed else jnp.zeros_like(mine_at), live_here]).astype(jnp.int32)

    def columns(matrix):
        return matrix.reshape(depth, -1, width).transpose(1, 0, 2).reshape(-1, width)

    qkv_scaled = (w_qkv[0].astype(F32) * gain_attn[0].astype(F32)[:, None]).astype(BF)
    up_scaled = (w_up[0].astype(F32) * gain_mlp[0].astype(F32)[:, None]).astype(BF)
    attn_own = jnp.concatenate([columns(qkv_scaled), w_out[0]]).reshape(2, 2 * depth, width)
    mlp_own = jnp.stack([columns(up_scaled), w_down[0]])

    def by_layer(own):
        kept, came = pick(own, me), swap_section(pick(own, 1 - me))
        return jnp.where(first, kept, came), jnp.where(first, came, kept)

    def spread(half, mlp):
        if packed:
            return [half] + exchange([half] * (shards - 1), "fsdp")
        full = lax.all_gather(half, "fsdp")
        blocks = full.reshape(shards, -1, depth, width).transpose(1, 0, 2, 3).reshape(-1, width)
        if mlp:
            blocks = jnp.where(first, blocks, full.reshape(-1, width))
        return [blocks]

    attn0, attn1 = by_layer(attn_own)
    attn0 = spread(attn0, False)
    mlp0, mlp1 = by_layer(mlp_own)
    came_images = swap_section(ends_in[0])
    images = [ends_in[0], came_images]
    attn0 = attn0 + [swap_section(p) for p in attn0]

    *tied, attn1, mlp0 = tie(*attn0, attn1, mlp0)
    attn0 = tied
    mlp0 = spread(mlp0, True)
    attn1 = spread(attn1, False)
    qkv0, probs0, mixt0, mid0, x0, weight0 = attn_fwd(ids, images, attn0, dims, True)

    np_ = len(mlp0)
    mid0, mlp1, *tied = tie(mid0, mlp1, *mlp0, *attn1)
    mlp0, attn1 = tied[:np_], tied[np_:]
    mlp0 = mlp0 + [swap_section(p) for p in mlp0]
    mlp1 = spread(mlp1, True)
    attn1 = attn1 + [swap_section(p) for p in attn1]
    x1, act0, slope0, up0, down0 = mlp_fwd(ids, mid0, mlp0, dims, False)

    x1, *tied = tie(x1, *attn1, *mlp1)
    attn1, mlp1 = tied[:2 * np_], tied[2 * np_:]
    mlp1 = mlp1 + [swap_section(p) for p in mlp1]
    qkv1, probs1, mixt1, mid1, x1, weight1 = attn_fwd(ids, x1, attn1, dims, False)
    mid1, *mlp1 = tie(mid1, *mlp1)
    out, act1, slope1, up1, down1 = mlp_fwd(ids, mid1, mlp1, dims, True)

    def scatter(half, came, mlp):
        if packed:
            parts = [total(half[k], [came[k]]) for k in range(count)]
            return [parts[0]] + exchange(parts[1:], "fsdp")
        chip = total(half, [came])
        blocks = chip.reshape(-1, shards, depth, width).transpose(1, 0, 2, 3).reshape(shards, -1, width)
        if mlp:
            blocks = jnp.where(first, blocks, chip.reshape(shards, -1, width))
        return [lax.psum_scatter(blocks, "fsdp", scatter_dimension=0)]

    def gather_sums(part):
        if direct(replicas):
            return [part] + exchange([part] * (replicas - 1), "replica")
        return [lax.psum(part, "replica")]

    def added(parts):
        return total(parts[0], parts[1:])

    gmid1, keep_m1, send_m1 = mlp_bwd(ids, images, mid1, act1, slope1, up1, down1, dims, count, True)
    came_m1 = swap_section(send_m1)
    came_out = swap_section(out)
    cot0, keep_a1, send_a1 = attn_bwd(ids, gmid1, x1, qkv1, probs1, mixt1, weight1, dims, count, False)

    cot0, came_m1, keep_m1, came_out = tie(cot0, came_m1, keep_m1, came_out)
    parts_m1 = scatter(keep_m1, came_m1, True)
    came_a1 = swap_section(send_a1)
    gmid0, keep_m0, send_m0 = mlp_bwd(ids, cot0, mid0, act0, slope0, up0, down0, dims, count, False)

    n1 = len(parts_m1)
    gmid0, came_a1, keep_a1, *parts_m1 = tie(gmid0, came_a1, keep_a1, *parts_m1)
    sums_m1 = gather_sums(added(parts_m1))
    parts_a1 = scatter(keep_a1, came_a1, False)
    came_m0 = swap_section(send_m0)
    gx, keep_a0, send_a0 = attn_bwd(ids, gmid0, x0, qkv0, probs0, mixt0, weight0, dims, count, True)

    nr = len(sums_m1)
    send_a0, gx, came_m0, keep_m0, *tied = tie(send_a0, gx, came_m0, keep_m0, *sums_m1, *parts_a1)
    sums_m1, parts_a1 = tied[:nr], tied[nr:]
    came_a0 = swap_section(send_a0)
    came_gx = swap_section(gx)
    parts_m0 = scatter(keep_m0, came_m0, True)
    sums_a1 = gather_sums(added(parts_a1))
    parts_a0 = scatter(keep_a0, came_a0, False)
    sums_m0 = gather_sums(added(parts_m0))
    sums_a0 = gather_sums(added(parts_a0))

    def own_layer(parts0, parts1):
        sum0, sum1 = added(parts0), added(parts1)
        mine = jnp.where(first, sum0, sum1)
        other = swap_section(jnp.where(first, sum1, sum0))
        return jnp.concatenate([jnp.where(first, mine, other), jnp.where(first, other, mine)]).astype(F32)

    mlp_grad = own_layer(sums_m0, sums_m1)
    attn_grad = own_layer(sums_a0, sums_a1)

    def rows_of(blocks):
        return blocks.reshape(-1, depth, width).transpose(1, 0, 2).reshape(depth, -1)

    def unscaled(grad, gain, weight):
        return (gain[0].astype(F32)[:, None] * grad)[None], jnp.sum(grad * weight[0].astype(F32), axis=-1)[None]

    grad_qkv, grad_gain_attn = unscaled(rows_of(attn_grad[:3 * depth]), gain_attn, w_qkv)
    grad_up, grad_gain_mlp = unscaled(rows_of(mlp_grad[:ff // width * depth]), gain_mlp, w_up)
    grad_out = attn_grad[3 * depth:][None]
    grad_down = mlp_grad[ratio * depth:][None]

    own = jnp.where(first, gx, out)
    came = jnp.where(first, came_gx, came_out)
    ends_out = jnp.where(first, jnp.concatenate([own, came]), jnp.concatenate([came, own]))
    return (ends_out[None], grad_gain_attn, grad_qkv, grad_out, grad_gain_mlp, grad_up, grad_down)


def solution(mesh):
    in_specs = (
        P("section", ("fsdp", "replica"), None, None),
        P(None, ("fsdp", "replica")),
        P("section", "fsdp"),
        P("section", "fsdp", None),
        P("section", "fsdp", None),
        P("section", "fsdp"),
        P("section", "fsdp", None),
        P("section", "fsdp", None),
    )
    out_specs = (
        P("section", ("fsdp", "replica"), None, None),
        P("section", "fsdp"),
        P("section", "fsdp", None),
        P("section", "fsdp", None),
        P("section", "fsdp"),
        P("section", "fsdp", None),
        P("section", "fsdp", None),
    )
    return jax.shard_map(local, mesh=mesh, in_specs=in_specs, out_specs=out_specs, check_vma=False)
```

time: 419 us -> 331 us (0.79)
  local copies, waits for them, and re-layouts: 67.8 us -> 11.2 us
  waiting for transfers between devices: 80.2 us -> 56.4 us
  Pallas kernels: 168 us -> 179 us
  other arithmetic: 24.2 us -> 15 us
  starting transfers between devices: 70.3 us -> 61.4 us
    ppermute x39 -> x36, waiting for transfers between devices: 77.5 us -> 51.7 us  [exchange(): lax.ppermute(v, axis, [(i, i ^ k + 1) for i in range(size)])]
    reshape x16 -> x3, local copies, waits for them, and re-layouts: 18.3 us -> 3.42 us  [rows_of(): blocks.reshape(-1, depth, width).transpose(1, 0, 2).reshape(depth, -1)]
    pallas_call x8, Pallas kernels: 168 us -> 179 us  [call(): pl.pallas_call(body, name=name, grid_spec=pltpu.PrefetchScalarGridSpec(nu...]
    dynamic_update_slice x24 -> x0, local copies, waits for them, and re-layouts: 9.61 us -> none  [the longest x3 3.26 us: gather_group(): both = lax.dynamic_update_index_in_dim(both, other, 1 - me, 0)]
    transpose x11 -> x2, local copies, waits for them, and re-layouts: 10.7 us -> 1.22 us  [the longest x1 1.2 us: rows_of(): blocks.reshape(-1, depth, width).transpose(1, 0, 2).reshape(depth, -1)]
    squeeze x8 -> x0, local copies, waits for them, and re-layouts: 6.64 us -> none  [the longest x2 3.41 us: attn_weights(): return (blocks[:3].transpose(1, 0, 2).reshape(width, 3 * width), blocks[3])]
    ppermute x15 -> x27, starting transfers between devices: 31.2 us -> 25 us  [swap_section(): return lax.ppermute(value, 'section', [(0, 1), (1, 0)])]
    convert_element_type x8 -> x11, other arithmetic: 7.66 us -> 2.07 us  [the longest x8 1.3 us: total(): return result.astype(BF)]
  transfers between devices with their start and end apart: 54 -> 63, of which waited for: 22 -> 16; matrix products, arithmetic and copies ran while one was open for 17% -> 6% of each run, Pallas kernels for 17% -> 51%
where the time goes in v2:
time: 331 us; the launch traced here: 325 us
  Pallas kernels  179 us (54%)
  starting transfers between devices  61.4 us (19%)
  waiting for transfers between devices  56.4 us (17%)
  other arithmetic  15 us (5%)
  local copies, waits for them, and re-layouts  11.2 us (3%)
    pallas_call x8, Pallas kernels, call(): pl.pallas_call(body, name=name, grid_spec=pltpu.PrefetchScalarGridSpec(nu...  179 us
    ppermute x36, waiting for transfers between devices, exchange(): lax.ppermute(v, axis, [(i, i ^ k + 1) for i in range(size)])  51.7 us
    ppermute x36, starting transfers between devices, exchange(): lax.ppermute(v, axis, [(i, i ^ k + 1) for i in range(size)])  36.4 us
    ppermute x27, starting transfers between devices, swap_section(): return lax.ppermute(value, 'section', [(0, 1), (1, 0)])  25 us
  transfers between devices with their start and end apart: 63, of which 16 were waited for; matrix products, arithmetic and copies ran while one was open for 6% of the time, Pallas kernels for 51%

profile of v2, /device:TPU:13, one launch (start us, length us, event | category | flops | bytes accessed | tf_op | source)
XLA Modules:
  0.0 324.7 jit_solution(2619311496463801658)
XLA Ops:
  4.7 2.1 collective-permute-done.1
  9.6 3.4 %collective-permute-done.4.refs_5_ = bf16[192,384]{1,0:T(8,128)(2,1)S(1)} collective-permute-done((bf16[192,384]{1,0:T(8,128)(2,1)S(1)}, bf16[192,384]{1,0:T(8,128)(2,1)S(1)}, u32[]{:S(2)}, u32[]{:S(2)}) %collective-permute-start.4) | collective-permute-done | bytes 147488 | tf_op jit(solution)/shard_map/ppermute | solution.py:396
  27.0 22.6 %attention_forward.2 = (bf16[10,208,1152]{2,1,0:T(8,128)(2,1)}, bf16[10,6,208,208]{3,2,1,0:T(8,128)(2,1)}, bf16[10,384,208]{2,1,0:T(8,128)(2,1)}, f32[10,208,384...) custom-call(s32[3]{0:T(128)} %pad_add_fusion.ids_ref, bf16[20,197,384]{2,1,0:T(8,128)(2,1)} %bitcast.102, ...), custom_call_target="tpu_custom_call" | custom-call | flops 3118202880 | bytes 18733056 | tf_op jit(solution)/shard_map/attention_forward/pallas_call | solution.py:307
  49.7 2.6 collective-permute-start.20
  59.8 14.9 %mlp_forward.2 = (bf16[10,208,384]{2,1,0:T(8,128)(2,1)}, bf16[10,208,1536]{2,1,0:T(8,128)(2,1)}, bf16[10,208,1536]{2,1,0:T(8,128)(2,1)}, bf16[384,1536]{1,0:T(8,128)(2,1)}, bf16[1536,384]{1,0:T(8,128)(2,1)}) custom-call(s32[3]{0:T(128)} %pad_add_fusion.ids_ref, f32[10,208,384]{2,1,0:T(8,128)} %get-tuple-element.116.mid_ref.refs_1_, ...), custom_call_target="tpu_custom_call" | custom-call | flops 4907335680 | bytes 22290432 | tf_op jit(solution)/shard_map/mlp_forward/pallas_call | solution.py:307
  76.0 21.7 %attention_forward.3 = (bf16[10,208,1152]{2,1,0:T(8,128)(2,1)}, bf16[10,6,208,208]{3,2,1,0:T(8,128)(2,1)}, bf16[10,384,208]{2,1,0:T(8,128)(2,1)}, f32[10,208,384]{2,1,0:T(8,128)}, bf16[384,1536]{1,0:T(8,128)(2,1)}) custom-call(s32[3]{0:T(128)} %pad_add_fusion.ids_ref, bf16[10,208,384]{2,1,0:T(8,128)(2,1)} %get-tuple-element.127.refs_0_.x_ref, ...), custom_call_target="tpu_custom_call" | custom-call | flops 3118202880 | bytes 18733056 | tf_op jit(solution)/shard_map/attention_forward/pallas_call | solution.py:307
  98.7 14.9 %mlp_forward.3 = (bf16[10,197,384]{2,1,0:T(8,128)(2,1)}, bf16[10,208,1536]{2,1,0:T(8,128)(2,1)}, bf16[10,208,1536]{2,1,0:T(8,128)(2,1)}, bf16[384,1536]{1,0:T(8,128)(2,1)}, bf16[1536,384]{1,0:T(8,128)(2,1)}) custom-call(s32[3]{0:T(128)} %pad_add_fusion.ids_ref, f32[10,208,384]{2,1,0:T(8,128)} %get-tuple-element.141.mid_ref.refs_2_, ...), custom_call_target="tpu_custom_call" | custom-call | flops 4907335680 | bytes 22205952 | tf_op jit(solution)/shard_map/mlp_forward/pallas_call | solution.py:307
  113.8 22.3 %mlp_backward.2 = (f32[10,208,384]{2,1,0:T(8,128)}, bf16[4,384,384]{2,1,0:T(8,128)(2,1)}, bf16[4,384,384]{2,1,0:T(8,128)(2,1)}) custom-call(s32[3]{0:T(128)} %pad_add_fusion.ids_ref, bf16[20,197,384]{2,1,0:T(8,128)(2,1)} %bitcast.103, bf16[20,197,384]{2,1,0:T(8,128)(2,1)} %collective-permute-done.refs_1_, ...), custom_call_target="tpu_custom_call" | custom-call | flops 9814671360 | bytes 23887872 | tf_op jit(solution)/shard_map/mlp_backward/pallas_call | solution.py:307
  136.5 30.3 %attention_backward.2 = (bf16[10,208,384]{2,1,0:T(8,128)(2,1)}, bf16[4,192,384]{2,1,0:T(8,128)(2,1)}, bf16[4,192,384]{2,1,0:T(8,128)(2,1)}) custom-call(s32[3]{0:T(128)} %pad_add_fusion.ids_ref, f32[10,208,384]{2,1,0:T(8,128)} %get-tuple-element.154.gmid_ref, bf16[10,208,384]{2,1,0:T(8,128)(2,1)} %get-tuple-element.127.refs_0_.x_ref, ...), custom_call_target="tpu_custom_call" | custom-call | flops 6568673280 | bytes 20330496 | tf_op jit(solution)/shard_map/attention_backward/pallas_call | solution.py:307
  170.7 22.0 %mlp_backward.3 = (f32[10,208,384]{2,1,0:T(8,128)}, bf16[4,384,384]{2,1,0:T(8,128)(2,1)}, bf16[4,384,384]{2,1,0:T(8,128)(2,1)}) custom-call(s32[3]{0:T(128)} %pad_add_fusion.ids_ref, bf16[10,208,384]{2,1,0:T(8,128)(2,1)} %get-tuple-element.163.refs_0_, f32[10,208,384]{2,1,0:T(8,128)} %get-tuple-element.116.mid_ref.refs_1_, ...), custom_call_target="tpu_custom_call" | custom-call | flops 9814671360 | bytes 25485312 | tf_op jit(solution)/shard_map/mlp_backward/pallas_call | solution.py:307
  198.3 2.3 collective-permute-done.43
  200.8 3.3 %collective-permute-done.42 = bf16[192,384]{1,0:T(8,128)(2,1)S(1)} collective-permute-done((bf16[192,384]{1,0:T(8,128)(2,1)S(1)}, bf16[192,384]{1,0:T(8,128)(2,1)S(1)}, u32[]{:S(2)}, u32[]{:S(2)}) %collective-permute-start.42) | collective-permute-done | bytes 147488 | tf_op jit(solution)/shard_map/ppermute | solution.py:396
  204.4 30.5 %attention_backward.3 = (bf16[10,197,384]{2,1,0:T(8,128)(2,1)}, bf16[4,192,384]{2,1,0:T(8,128)(2,1)}, bf16[4,192,384]{2,1,0:T(8,128)(2,1)}) custom-call(s32[3]{0:T(128)} %pad_add_fusion.ids_ref, f32[10,208,384]{2,1,0:T(8,128)} %get-tuple-element.173.gmid_ref, bf16[10,208,384]{2,1,0:T(8,128)(2,1)} %get-tuple-element.174.x_ref, ...), custom_call_target="tpu_custom_call" | custom-call | flops 6568673280 | bytes 20246016 | tf_op jit(solution)/shard_map/attention_backward/pallas_call | solution.py:307
  239.5 3.5 %collective-permute-done.56 = bf16[384,384]{1,0:T(8,128)(2,1)S(1)} collective-permute-done((bf16[384,384]{1,0:T(8,128)(2,1)S(1)}, bf16[384,384]{1,0:T(8,128)(2,1)S(1)}, u32[]{:S(2)}, u32[]{:S(2)}) %collective-permute-start.56) | collective-permute-done | bytes 294944 | tf_op jit(solution)/shard_map/ppermute | solution.py:396
  243.0 7.3 %collective-permute-done.58 = bf16[384,384]{1,0:T(8,128)(2,1)S(1)} collective-permute-done((bf16[384,384]{1,0:T(8,128)(2,1)S(1)}, bf16[384,384]{1,0:T(8,128)(2,1)S(1)}, u32[]{:S(2)}, u32[]{:S(2)}) %collective-permute-start.58) | collective-permute-done | bytes 294944 | tf_op jit(solution)/shard_map/ppermute | solution.py:396
  256.8 16.0 %collective-permute-done.61 = bf16[384,384]{1,0:T(8,128)(2,1)S(1)} collective-permute-done((bf16[384,384]{1,0:T(8,128)(2,1)S(1)}, bf16[384,384]{1,0:T(8,128)(2,1)S(1)}, u32[]{:S(2)}, u32[]{:S(2)}) %collective-permute-start.61) | collective-permute-done | bytes 294944 | tf_op jit(solution)/shard_map/ppermute | solution.py:396
  273.4 8.6 %collective-permute-done.60 = bf16[384,384]{1,0:T(8,128)(2,1)S(1)} collective-permute-done((bf16[384,384]{1,0:T(8,128)(2,1)S(1)}, bf16[384,384]{1,0:T(8,128)(2,1)S(1)}, u32[]{:S(2)}, u32[]{:S(2)}) %collective-permute-start.60) | collective-permute-done | bytes 294944 | tf_op jit(solution)/shard_map/ppermute | solution.py:396
  284.1 3.2 collective-permute-start.52
  287.3 5.3 %collective-permute-start.62 = (bf16[384,384]{1,0:T(8,128)(2,1)S(1)}, bf16[384,384]{1,0:T(8,128)(2,1)S(1)}, u32[]{:S(2)}, u32[]{:S(2)}) collective-permute-start(bf16[384,384]{1,0:T(8,128)(2,1)S(1)} %get-tuple-element.203), channel_id=1, source_target_pairs={{0,16},{16,0},{1,17},{17,1},{2,18},{18,2},{3,19},{19,3},{4,20},{20... | collective-permute-start | bytes 884744 | tf_op jit(solution)/shard_map/ppermute | solution.py:383
  293.0 3.0 collective-permute-start.50
  297.4 3.5 %collective-permute-start.44 = (bf16[10,197,384]{2,1,0:T(8,128)(2,1)}, bf16[10,197,384]{2,1,0:T(8,128)(2,1)}, u32[]{:S(2)}, u32[]{:S(2)}) collective-permute-start(bf16[10,197,384]{2,1,0:T(8,128)(2,1)} %get-tuple-element.189), channel_id=1, source_target_pairs={{0,16},{16,0},{1,17},{17,1},{2,18},{18,2},{3,19},{19,3},{4,20},{20... | collective-permute-start | bytes 4538888 | tf_op jit(solution)/shard_map/ppermute | solution.py:383
  300.9 3.6 %collective-permute-done.50 = bf16[192,384]{1,0:T(8,128)(2,1)S(1)} collective-permute-done((bf16[192,384]{1,0:T(8,128)(2,1)S(1)}, bf16[192,384]{1,0:T(8,128)(2,1)S(1)}, u32[]{:S(2)}, u32[]{:S(2)}) %collective-permute-start.50) | collective-permute-done | bytes 147488 | tf_op jit(solution)/shard_map/ppermute | solution.py:396
  306.8 2.3 collective-permute-start.55
  321.6 2.8 maximum_select_fusion
  (250 shorter events, 71.0 us)
Async XLA Ops:
  0.7 25.1 %collective-permute-start = (bf16[20,197,384]{2,1,0:T(8,128)(2,1)}, bf16[20,197,384]{2,1,0:T(8,128)(2,1)}, u32[]{:S(2)}, u32[]{:S(2)}) collective-permute-start(bf16[20,197,384]{2,1,0:T(8,128)(2,1)} %bitcast.101), channel_id=1, source_target_pairs={{0,16},{16,0},{1,17},{17,1},{2,18},{18,2},{3,19},{19,3},{4,20},{20... | collective-permute-start | bytes 9077768 | tf_op jit(solution)/shard_map/ppermute | solution.py:383
  21.2 28.4 %collective-permute-start.12 = (bf16[384,384]{1,0:T(8,128)(2,1)S(1)}, bf16[384,384]{1,0:T(8,128)(2,1)S(1)}, u32[]{:S(2)}, u32[]{:S(2)}) collective-permute-start(bf16[384,384]{1,0:T(8,128)(2,1)S(1)} %get-tuple-element.117.refs_0_), channel_id=1, source_target_pairs={{0,12},{4,8},{8,4},{12,0},{1,13},{5,9},{9,5},{13,1},{2,14},{6,10},... | collective-permute-start | bytes 884744 | tf_op jit(solution)/shard_map/ppermute | solution.py:396
  22.5 27.2 %collective-permute-start.11 = (bf16[384,384]{1,0:T(8,128)(2,1)S(1)}, bf16[384,384]{1,0:T(8,128)(2,1)S(1)}, u32[]{:S(2)}, u32[]{:S(2)}) collective-permute-start(bf16[384,384]{1,0:T(8,128)(2,1)S(1)} %get-tuple-element.117.refs_0_), channel_id=1, source_target_pairs={{0,8},{4,12},{8,0},{12,4},{1,9},{5,13},{9,1},{13,5},{2,10},{6,14},... | collective-permute-start | bytes 884744 | tf_op jit(solution)/shard_map/ppermute | solution.py:396
  22.7 27.0 %collective-permute-start.10 = (bf16[384,384]{1,0:T(8,128)(2,1)S(1)}, bf16[384,384]{1,0:T(8,128)(2,1)S(1)}, u32[]{:S(2)}, u32[]{:S(2)}) collective-permute-start(bf16[384,384]{1,0:T(8,128)(2,1)S(1)} %get-tuple-element.117.refs_0_), channel_id=1, source_target_pairs={{0,4},{4,0},{8,12},{12,8},{1,5},{5,1},{9,13},{13,9},{2,6},{6,2},{1... | collective-permute-start | bytes 884744 | tf_op jit(solution)/shard_map/ppermute | solution.py:396
  25.5 24.0 %collective-permute-start.14 = (bf16[192,384]{1,0:T(8,128)(2,1)S(1)}, bf16[192,384]{1,0:T(8,128)(2,1)S(1)}, u32[]{:S(2)}, u32[]{:S(2)}) collective-permute-start(bf16[192,384]{1,0:T(8,128)(2,1)S(1)} %get-tuple-element.128.refs_1_), channel_id=1, source_target_pairs={{0,8},{4,12},{8,0},{12,4},{1,9},{5,13},{9,1},{13,5},{2,10},{6,14},... | collective-permute-start | bytes 442376 | tf_op jit(solution)/shard_map/ppermute | solution.py:396
  25.8 23.8 %collective-permute-start.13 = (bf16[192,384]{1,0:T(8,128)(2,1)S(1)}, bf16[192,384]{1,0:T(8,128)(2,1)S(1)}, u32[]{:S(2)}, u32[]{:S(2)}) collective-permute-start(bf16[192,384]{1,0:T(8,128)(2,1)S(1)} %get-tuple-element.128.refs_1_), channel_id=1, source_target_pairs={{0,4},{4,0},{8,12},{12,8},{1,5},{5,1},{9,13},{13,9},{2,6},{6,2},{1... | collective-permute-start | bytes 442376 | tf_op jit(solution)/shard_map/ppermute | solution.py:396
  74.9 22.8 %collective-permute-start.27 = (bf16[384,384]{1,0:T(8,128)(2,1)S(1)}, bf16[384,384]{1,0:T(8,128)(2,1)S(1)}, u32[]{:S(2)}, u32[]{:S(2)}) collective-permute-start(bf16[384,384]{1,0:T(8,128)(2,1)S(1)} %get-tuple-element.142.refs_0_), channel_id=1, source_target_pairs={{0,16},{16,0},{1,17},{17,1},{2,18},{18,2},{3,19},{19,3},{4,20},{20... | collective-permute-start | bytes 884744 | tf_op jit(solution)/shard_map/ppermute | solution.py:383
  75.0 22.7 %collective-permute-start.28 = (bf16[384,384]{1,0:T(8,128)(2,1)S(1)}, bf16[384,384]{1,0:T(8,128)(2,1)S(1)}, u32[]{:S(2)}, u32[]{:S(2)}) collective-permute-start(bf16[384,384]{1,0:T(8,128)(2,1)S(1)} %collective-permute-done.24.refs_1_), channel_id=1, source_target_pairs={{0,16},{16,0},{1,17},{17,1},{2,18},{18,2},{3,19},{19,3},{4,20},{20... | collective-permute-start | bytes 884744 | tf_op jit(solution)/shard_map/ppermute | solution.py:383
  113.6 53.3 %collective-permute-start.32 = (bf16[10,197,384]{2,1,0:T(8,128)(2,1)}, bf16[10,197,384]{2,1,0:T(8,128)(2,1)S(1)}, u32[]{:S(2)}, u32[]{:S(2)}) collective-permute-start(bf16[10,197,384]{2,1,0:T(8,128)(2,1)} %get-tuple-element.162), channel_id=1, source_target_pairs={{0,16},{16,0},{1,17},{17,1},{2,18},{18,2},{3,19},{19,3},{4,20},{20... | collective-permute-start | bytes 4538888 | tf_op jit(solution)/shard_map/ppermute | solution.py:383
  136.1 30.9 %collective-permute-start.31 = (bf16[4,384,384]{2,1,0:T(8,128)(2,1)}, bf16[4,384,384]{2,1,0:T(8,128)(2,1)S(1)}, u32[]{:S(2)}, u32[]{:S(2)}) collective-permute-start(bf16[4,384,384]{2,1,0:T(8,128)(2,1)} %get-tuple-element.160), channel_id=1, source_target_pairs={{0,16},{16,0},{1,17},{17,1},{2,18},{18,2},{3,19},{19,3},{4,20},{20... | collective-permute-start | bytes 3538952 | tf_op jit(solution)/shard_map/ppermute | solution.py:383
  166.8 27.2 %collective-permute-start.33 = (bf16[4,192,384]{2,1,0:T(8,128)(2,1)}, bf16[4,192,384]{2,1,0:T(8,128)(2,1)S(1)}, u32[]{:S(2)}, u32[]{:S(2)}) collective-permute-start(bf16[4,192,384]{2,1,0:T(8,128)(2,1)} %get-tuple-element.169), channel_id=1, source_target_pairs={{0,16},{16,0},{1,17},{17,1},{2,18},{18,2},{3,19},{19,3},{4,20},{20... | collective-permute-start | bytes 1769480 | tf_op jit(solution)/shard_map/ppermute | solution.py:383
  168.0 25.9 %collective-permute-start.36 = (bf16[384,384]{1,0:T(8,128)(2,1)S(1)}, bf16[384,384]{1,0:T(8,128)(2,1)S(1)}, u32[]{:S(2)}, u32[]{:S(2)}) collective-permute-start(bf16[384,384]{1,0:T(8,128)(2,1)S(1)} %get-tuple-element.212), channel_id=1, source_target_pairs={{0,12},{4,8},{8,4},{12,0},{1,13},{5,9},{9,5},{13,1},{2,14},{6,10},... | collective-permute-start | bytes 884744 | tf_op jit(solution)/shard_map/ppermute | solution.py:396
  169.2 24.8 %collective-permute-start.35 = (bf16[384,384]{1,0:T(8,128)(2,1)S(1)}, bf16[384,384]{1,0:T(8,128)(2,1)S(1)}, u32[]{:S(2)}, u32[]{:S(2)}) collective-permute-start(bf16[384,384]{1,0:T(8,128)(2,1)S(1)} %get-tuple-element.213), channel_id=1, source_target_pairs={{0,8},{4,12},{8,0},{12,4},{1,9},{5,13},{9,1},{13,5},{2,10},{6,14},... | collective-permute-start | bytes 884744 | tf_op jit(solution)/shard_map/ppermute | solution.py:396
  169.5 24.5 %collective-permute-start.34 = (bf16[384,384]{1,0:T(8,128)(2,1)S(1)}, bf16[384,384]{1,0:T(8,128)(2,1)S(1)}, u32[]{:S(2)}, u32[]{:S(2)}) collective-permute-start(bf16[384,384]{1,0:T(8,128)(2,1)S(1)} %get-tuple-element.214), channel_id=1, source_target_pairs={{0,4},{4,0},{8,12},{12,8},{1,5},{5,1},{9,13},{13,9},{2,6},{6,2},{1... | collective-permute-start | bytes 884744 | tf_op jit(solution)/shard_map/ppermute | solution.py:396
  192.7 42.2 %collective-permute-start.37 = (bf16[4,384,384]{2,1,0:T(8,128)(2,1)}, bf16[4,384,384]{2,1,0:T(8,128)(2,1)S(1)}, u32[]{:S(2)}, u32[]{:S(2)}) collective-permute-start(bf16[4,384,384]{2,1,0:T(8,128)(2,1)} %get-tuple-element.181), channel_id=1, source_target_pairs={{0,16},{16,0},{1,17},{17,1},{2,18},{18,2},{3,19},{19,3},{4,20},{20... | collective-permute-start | bytes 3538952 | tf_op jit(solution)/shard_map/ppermute | solution.py:383
  195.8 39.0 %collective-permute-start.40 = (bf16[384,384]{1,0:T(8,128)(2,1)S(1)}, bf16[384,384]{1,0:T(8,128)(2,1)S(1)}, u32[]{:S(2)}, u32[]{:S(2)}) collective-permute-start(bf16[384,384]{1,0:T(8,128)(2,1)S(1)} %add_convert_fusion.6), channel_id=1, source_target_pairs={{0,3},{1,2},{2,1},{3,0},{4,7},{5,6},{6,5},{7,4},{8,11},{9,10},{10,... | collective-permute-start | bytes 884744 | tf_op jit(solution)/shard_map/ppermute | solution.py:396
  197.2 37.7 %collective-permute-start.39 = (bf16[384,384]{1,0:T(8,128)(2,1)S(1)}, bf16[384,384]{1,0:T(8,128)(2,1)S(1)}, u32[]{:S(2)}, u32[]{:S(2)}) collective-permute-start(bf16[384,384]{1,0:T(8,128)(2,1)S(1)} %add_convert_fusion.6), channel_id=1, source_target_pairs={{0,2},{1,3},{2,0},{3,1},{4,6},{5,7},{6,4},{7,5},{8,10},{9,11},{10,... | collective-permute-start | bytes 884744 | tf_op jit(solution)/shard_map/ppermute | solution.py:396
  200.6 34.3 %collective-permute-start.38 = (bf16[384,384]{1,0:T(8,128)(2,1)S(1)}, bf16[384,384]{1,0:T(8,128)(2,1)S(1)}, u32[]{:S(2)}, u32[]{:S(2)}) collective-permute-start(bf16[384,384]{1,0:T(8,128)(2,1)S(1)} %add_convert_fusion.6), channel_id=1, source_target_pairs={{0,1},{1,0},{2,3},{3,2},{4,5},{5,4},{6,7},{7,6},{8,9},{9,8},{10,11... | collective-permute-start | bytes 884744 | tf_op jit(solution)/shard_map/ppermute | solution.py:396
  204.1 30.8 %collective-permute-start.41 = (bf16[192,384]{1,0:T(8,128)(2,1)S(1)}, bf16[192,384]{1,0:T(8,128)(2,1)S(1)}, u32[]{:S(2)}, u32[]{:S(2)}) collective-permute-start(bf16[192,384]{1,0:T(8,128)(2,1)S(1)} %get-tuple-element.223), channel_id=1, source_target_pairs={{0,4},{4,0},{8,12},{12,8},{1,5},{5,1},{9,13},{13,9},{2,6},{6,2},{1... | collective-permute-start | bytes 442376 | tf_op jit(solution)/shard_map/ppermute | solution.py:396
  251.9 30.0 %collective-permute-start.60 = (bf16[384,384]{1,0:T(8,128)(2,1)S(1)}, bf16[384,384]{1,0:T(8,128)(2,1)S(1)}, u32[]{:S(2)}, u32[]{:S(2)}) collective-permute-start(bf16[384,384]{1,0:T(8,128)(2,1)S(1)} %fusion.2), channel_id=1, source_target_pairs={{0,2},{1,3},{2,0},{3,1},{4,6},{5,7},{6,4},{7,5},{8,10},{9,11},{10,... | collective-permute-start | bytes 884744 | tf_op jit(solution)/shard_map/ppermute | solution.py:396
  253.0 30.1 %collective-permute-start.59 = (bf16[384,384]{1,0:T(8,128)(2,1)S(1)}, bf16[384,384]{1,0:T(8,128)(2,1)S(1)}, u32[]{:S(2)}, u32[]{:S(2)}) collective-permute-start(bf16[384,384]{1,0:T(8,128)(2,1)S(1)} %fusion.2), channel_id=1, source_target_pairs={{0,1},{1,0},{2,3},{3,2},{4,5},{5,4},{6,7},{7,6},{8,9},{9,8},{10,11... | collective-permute-start | bytes 884744 | tf_op jit(solution)/shard_map/ppermute | solution.py:396
  254.2 38.8 %collective-permute-start.54 = (bf16[192,384]{1,0:T(8,128)(2,1)S(1)}, bf16[192,384]{1,0:T(8,128)(2,1)S(1)}, u32[]{:S(2)}, u32[]{:S(2)}) collective-permute-start(bf16[192,384]{1,0:T(8,128)(2,1)S(1)} %add_convert_fusion.12), channel_id=1, source_target_pairs={{0,3},{1,2},{2,1},{3,0},{4,7},{5,6},{6,5},{7,4},{8,11},{9,10},{10,... | collective-permute-start | bytes 442376 | tf_op jit(solution)/shard_map/ppermute | solution.py:396
  255.4 40.6 %collective-permute-start.53 = (bf16[192,384]{1,0:T(8,128)(2,1)S(1)}, bf16[192,384]{1,0:T(8,128)(2,1)S(1)}, u32[]{:S(2)}, u32[]{:S(2)}) collective-permute-start(bf16[192,384]{1,0:T(8,128)(2,1)S(1)} %add_convert_fusion.12), channel_id=1, source_target_pairs={{0,2},{1,3},{2,0},{3,1},{4,6},{5,7},{6,4},{7,5},{8,10},{9,11},{10,... | collective-permute-start | bytes 442376 | tf_op jit(solution)/shard_map/ppermute | solution.py:396
  297.4 24.1 %collective-permute-start.44 = (bf16[10,197,384]{2,1,0:T(8,128)(2,1)}, bf16[10,197,384]{2,1,0:T(8,128)(2,1)}, u32[]{:S(2)}, u32[]{:S(2)}) collective-permute-start(bf16[10,197,384]{2,1,0:T(8,128)(2,1)} %get-tuple-element.189), channel_id=1, source_target_pairs={{0,16},{16,0},{1,17},{17,1},{2,18},{18,2},{3,19},{19,3},{4,20},{20... | collective-permute-start | bytes 4538888 | tf_op jit(solution)/shard_map/ppermute | solution.py:383
  (88 other events, 971.8 us)
